TPU v7x, 32 devices: a whole 2x2x4 slice. The times are simulated.
32 devices in a mesh: seq: 16 (over z, y, x), mp: 2 (over core).
Axes of the slice: x: 2, y: 2, z: 4, core: 2. Of those that a mesh axis runs over, the one named last changes fastest.
Arguments:
- byte_state: bfloat16 [16384, 1024], P('seq'), may hold values from -6 to 6
- patch_id: int32 [16384], P('seq'), may hold values from 0 to 3583, as said below
- w_query: bfloat16 [1024, 1024], P('seq', 'mp'), may hold values from -0.1875 to 0.1875
- w_key: bfloat16 [1024, 1024], P('seq', 'mp'), may hold values from -0.1875 to 0.1875
- w_value: bfloat16 [1024, 1024], P('seq', 'mp'), may hold values from -0.1875 to 0.1875
- w_out: bfloat16 [1024, 4096], P('seq', 'mp'), may hold values from -0.1875 to 0.1875
- out_grad: bfloat16 [3584, 4096], P('seq', 'mp'), may hold values from -6 to 6
Outputs:
- patch_embed: bfloat16 [3584, 4096], P('seq', 'mp')
- byte_grad: bfloat16 [16384, 1024], P('seq')
- grad_query: float32 [1024, 1024], P('seq', 'mp')
- grad_key: float32 [1024, 1024], P('seq', 'mp')
- grad_value: float32 [1024, 1024], P('seq', 'mp')
- grad_out: float32 [1024, 4096], P('seq', 'mp')
Inputs may be any that keep to these rules, and one draw needn't show every extreme that they name: `patch_id`: never falls along the bytes; every patch has 1 to 16 bytes, all on one index of seq, and the first patch on each index has exactly 16. The first patch of the bytes of index s is numbered 224 * s plus an offset of 1 to 56; the offset is 0 on index 0 and 56 on some index; the last index ends with patch 3584 - 1.
All inputs are finite; a program needn't handle non-finite values.
Results may differ from a plain program's by a relative error of at most 0.002.
The roundings to bfloat16 on the way count: a program that leaves them out, or rounds other values in their place, can miss the bound.
Values may be sent and summed in bfloat16 or wider, within the bound.
A program may use at most 128 MiB of HBM per device.

v0:
```python
import jax
import jax.numpy as jnp
from jax import lax
from jax.sharding import PartitionSpec as P

HEAD = 64
DRIFT = 56
SLOTS = 280


def passed_along(value, axis, steps):
    count = lax.axis_size(axis)
    initial, last = (max(0, -steps), min(count, count - steps))
    return lax.ppermute(value, axis, [(source, source + steps) for source in range(initial, last)])


def contract_cols(left_side, right_side):
    return lax.dot_general(
        left_side, right_side, (((1,), (1,)), ((), ())), preferred_element_type=jnp.float32
    )


def contract_rows(left_side, right_side):
    return lax.dot_general(
        left_side, right_side, (((0,), (0,)), ((), ())), preferred_element_type=jnp.float32
    )


def local(byte_state, patch_id, w_query, w_key, w_value, w_out, out_grad):
    seq_rank = lax.axis_index("seq")
    model_rank = lax.axis_index("mp")
    width_cols = w_query.shape[1]
    group_heads = width_cols // HEAD
    patch_rows = out_grad.shape[0]
    byte_rows = byte_state.shape[0]
    score_scale = HEAD ** (-0.5)
    full_query, full_key, full_value, full_out = (
        lax.all_gather(w_query, "seq", axis=0, tiled=True),
        lax.all_gather(w_key, "seq", axis=0, tiled=True),
        lax.all_gather(w_value, "seq", axis=0, tiled=True),
        lax.all_gather(w_out, "seq", axis=0, tiled=True),
    )
    kv_weight = jnp.concatenate([full_key, full_value], axis=1)
    keyval = jnp.dot(byte_state, kv_weight, preferred_element_type=jnp.float32).astype(jnp.bfloat16)
    key_heads = keyval[:, :width_cols].reshape(byte_rows, group_heads, HEAD)
    value_heads = keyval[:, width_cols:].reshape(byte_rows, group_heads, HEAD)
    first_patch = patch_id[0]
    last_patch = patch_id[byte_rows - 1]
    slot_index = jnp.arange(SLOTS, dtype=jnp.int32)
    member = (patch_id - first_patch)[None, :] == slot_index[:, None]
    member_half = member.astype(jnp.bfloat16)
    length = jnp.maximum(jnp.sum(member.astype(jnp.float32), axis=1), 1.0)
    pooled = (
        jnp.dot(member_half, byte_state, preferred_element_type=jnp.float32) / length[:, None]
    ).astype(jnp.bfloat16)
    query_proj = jnp.dot(pooled, full_query, preferred_element_type=jnp.float32).astype(
        jnp.bfloat16
    )
    query_heads = query_proj.reshape(SLOTS, group_heads, HEAD)
    scores = (
        jnp.einsum("shd,bhd->hsb", query_heads, key_heads, preferred_element_type=jnp.float32)
        * score_scale
    )
    masked = jnp.where(member[None], scores, -1e30)
    peak = jnp.max(masked, axis=2, keepdims=True)
    exp_terms = jnp.where(member[None], jnp.exp(masked - peak), 0.0)
    prob_float = exp_terms / jnp.maximum(jnp.sum(exp_terms, axis=2, keepdims=True), 1.0)
    prob_half = prob_float.astype(jnp.bfloat16)
    attended = jnp.einsum(
        "hsb,bhd->shd", prob_half, value_heads, preferred_element_type=jnp.float32
    )
    attended = attended.reshape(SLOTS, width_cols).astype(jnp.bfloat16)
    target_row = first_patch - seq_rank * patch_rows + slot_index
    slot_live = slot_index <= last_patch - first_patch
    own_map = (
        (target_row[None, :] == jnp.arange(patch_rows, dtype=jnp.int32)[:, None])
        & slot_live[None, :]
    ).astype(jnp.bfloat16)
    next_map = (
        (target_row[None, :] - patch_rows == jnp.arange(DRIFT, dtype=jnp.int32)[:, None])
        & slot_live[None, :]
    ).astype(jnp.bfloat16)
    outgoing = jnp.dot(next_map, attended, preferred_element_type=jnp.float32).astype(jnp.bfloat16)
    incoming = passed_along(outgoing, "seq", 1)
    own_block = jnp.dot(own_map, attended, preferred_element_type=jnp.float32)
    own_block = (
        own_block + jnp.pad(incoming.astype(jnp.float32), ((0, patch_rows - DRIFT), (0, 0)))
    ).astype(jnp.bfloat16)
    heads_all = lax.all_gather(own_block, "mp", axis=1, tiled=True)
    patch_embed = jnp.dot(heads_all, full_out, preferred_element_type=jnp.float32).astype(
        jnp.bfloat16
    )
    partial_sum = contract_cols(out_grad, full_out)
    head_totals = lax.psum(partial_sum.astype(jnp.bfloat16), "mp").astype(jnp.float32)
    head_grad = lax.dynamic_slice_in_dim(
        head_totals, model_rank * width_cols, width_cols, 1
    ).astype(jnp.bfloat16)
    grad_out = contract_rows(heads_all, out_grad)
    returned = passed_along(head_grad[:DRIFT], "seq", -1)
    slot_grad = (contract_rows(own_map, head_grad) + contract_rows(next_map, returned)).astype(
        jnp.bfloat16
    )
    slot_heads = slot_grad.reshape(SLOTS, group_heads, HEAD)
    prob_grad = jnp.einsum(
        "shd,bhd->hsb", slot_heads, value_heads, preferred_element_type=jnp.float32
    )
    value_grad = jnp.einsum(
        "hsb,shd->bhd", prob_half, slot_heads, preferred_element_type=jnp.float32
    )
    value_grad = value_grad.reshape(byte_rows, width_cols).astype(jnp.bfloat16)
    score_grad = (
        prob_float
        * (prob_grad - jnp.sum(prob_float * prob_grad, axis=2, keepdims=True))
        * score_scale
    )
    score_grad = score_grad.astype(jnp.bfloat16)
    query_grad = jnp.einsum(
        "hsb,bhd->shd", score_grad, key_heads, preferred_element_type=jnp.float32
    )
    query_grad = query_grad.reshape(SLOTS, width_cols).astype(jnp.bfloat16)
    key_grad = jnp.einsum(
        "hsb,shd->bhd", score_grad, query_heads, preferred_element_type=jnp.float32
    )
    key_grad = key_grad.reshape(byte_rows, width_cols).astype(jnp.bfloat16)
    grad_query = contract_rows(pooled, query_grad)
    keyval_grad = jnp.concatenate([key_grad, value_grad], axis=1)
    grad_keyval = contract_rows(byte_state, keyval_grad)
    grad_key = grad_keyval[:, :width_cols]
    grad_value = grad_keyval[:, width_cols:]
    pooled_grad = (contract_cols(query_grad, full_query) / length[:, None]).astype(jnp.bfloat16)
    byte_part = contract_cols(keyval_grad, kv_weight) + contract_rows(member_half, pooled_grad)
    byte_grad = lax.psum(byte_part.astype(jnp.bfloat16), "mp")
    grad_query, grad_key, grad_value, grad_out = (
        lax.psum_scatter(grad_query, "seq", scatter_dimension=0, tiled=True),
        lax.psum_scatter(grad_key, "seq", scatter_dimension=0, tiled=True),
        lax.psum_scatter(grad_value, "seq", scatter_dimension=0, tiled=True),
        lax.psum_scatter(grad_out, "seq", scatter_dimension=0, tiled=True),
    )
    return (patch_embed, byte_grad, grad_query, grad_key, grad_value, grad_out)


def solution(mesh):
    in_specs = (
        P("seq", None),
        P("seq"),
        P("seq", "mp"),
        P("seq", "mp"),
        P("seq", "mp"),
        P("seq", "mp"),
        P("seq", "mp"),
    )
    out_specs = (
        P("seq", "mp"),
        P("seq", None),
        P("seq", "mp"),
        P("seq", "mp"),
        P("seq", "mp"),
        P("seq", "mp"),
    )
    return jax.shard_map(local, mesh=mesh, in_specs=in_specs, out_specs=out_specs, check_vma=False)
```

profile of v0, /device:TPU:0, one launch (start us, length us, event | category | flops | bytes accessed | tf_op | source)
XLA Modules:
  0.0 818.5 jit_solution(6204701497347057248)
XLA Ops:
  16.6 52.2 %all-gather.9.cloned.1.call-done = bf16[1024,512]{1,0:T(8,128)(2,1)} async-done(((bf16[64,512]{1,0:T(8,128)(2,1)}), bf16[1024,512]{1,0:T(8,128)(2,1)}) %all-gather.9.cloned.1.call-update) | async-done | bytes 1048592 | tf_op jit(solution)/shard_map/all_gather | solution.py:38
  70.7 54.9 %all-gather.5.cloned.1.call-done = bf16[1024,512]{1,0:T(8,128)(2,1)} async-done(((bf16[64,512]{1,0:T(8,128)(2,1)}), bf16[1024,512]{1,0:T(8,128)(2,1)}) %all-gather.5.cloned.1.call-update) | async-done | bytes 1048592 | tf_op jit(solution)/shard_map/all_gather | solution.py:39
  127.9 54.6 %all-gather.7.cloned.1.call-done = bf16[1024,512]{1,0:T(8,128)(2,1)} async-done(((bf16[64,512]{1,0:T(8,128)(2,1)}), bf16[1024,512]{1,0:T(8,128)(2,1)}) %all-gather.7.cloned.1.call-update) | async-done | bytes 1048592 | tf_op jit(solution)/shard_map/all_gather | solution.py:40
  184.8 4.0 convert_bitcast_fusion
  190.0 70.1 %all-gather.11.cloned.1.call-done = bf16[1024,2048]{1,0:T(8,128)(2,1)} async-done(((bf16[64,2048]{1,0:T(8,128)(2,1)}), bf16[1024,2048]{1,0:T(8,128)(2,1)}) %all-gather.11.cloned.1.call-update) | async-done | bytes 4194320 | tf_op jit(solution)/shard_map/all_gather | solution.py:41
  260.1 4.7 convolution_convert_fusion.1
  264.8 9.5 %fusion.69 = (f32[8,280]{1,0:T(8,128)}, f32[8,280,1024]{2,1,0:T(8,128)}) fusion(pred[280,1024]{1,0:T(8,128)(4,1)} %iota_compare_fusion, bf16[280,8,64]{0,2,1:T(8,128)(2,1)S(1)} %bitcast.65, bf16[1024,8,64]{0,2,1:T(8,128)(2,1)} %bitcast.59), kind=kOutput, calls=%fused_computation.78 | convolution fusion | flops 305071104 | bytes 10806016 | tf_op jit(solution)/shard_map/sub | solution.py:66
  275.6 6.5 all-reduce.4.cloned.1.call-done
  284.9 4.3 collective-permute-done.1
  291.4 5.9 fusion.70
  300.5 23.7 %fusion.31 = bf16[8,64,280]{2,1,0:T(8,128)(2,1)S(1)} fusion(bf16[1024,8,64]{0,2,1:T(8,128)(2,1)} %bitcast.60, f32[8,280,1024]{2,1,0:T(8,128)} %fusion.70, f32[8,280,1024]{2,1,0:T(8,128)} %get-tuple-element.31, f32[8,280]{1,0:T(8,128)} %broadcast_maximum_fusion), kind=kOutput, calls=%fused_computation.32 | convolution fusion | flops 309804224 | bytes 19694336 | tf_op jit(solution)/shard_map/hsb,bhd->shd/dot_general | solution.py:117
  324.2 25.0 %fusion.22 = bf16[8,64,1024]{2,1,0:T(8,128)(2,1)} fusion(bf16[280,8,64]{0,2,1:T(8,128)(2,1)} %bitcast.66, f32[8,280,1024]{2,1,0:T(8,128)} %fusion.70, f32[8,280,1024]{2,1,0:T(8,128)} %get-tuple-element.31, f32[8,280]{1,0:T(8,128)} %broadcast_maximum_fusion), kind=kOutput, calls=%fused_computation.24 | convolution fusion | flops 310185152 | bytes 19694336 | tf_op jit(solution)/shard_map/hsb,shd->bhd/dot_general | solution.py:121
  349.2 6.7 fusion.25
  355.9 5.6 add_convert_fusion
  361.6 3.2 fusion.71
  365.1 3.9 convolution_bitcast_fusion
  377.4 5.6 fusion.28
  383.3 4.8 collective-permute-start
  392.3 4.5 fusion.72
  396.9 4.2 convolution_convert_fusion
  401.1 68.4 %reduce-scatter.9.cloned.1.call-done = f32[64,512]{1,0:T(8,128)} async-done(((f32[1024,512]{1,0:T(8,128)}), f32[64,512]{1,0:T(8,128)}) %reduce-scatter.9.cloned.1.call-update) | async-done | bytes 131088 | tf_op jit(solution)/shard_map/reduce_scatter | solution.py:134
  469.5 80.7 %reduce-scatter.15.cloned.1.call-done = f32[64,512]{1,0:T(8,128)} async-done(((f32[1024,512]{1,0:T(8,128)}), f32[64,512]{1,0:T(8,128)}) %reduce-scatter.15.cloned.1.call-update) | async-done | bytes 131088
  550.3 80.6 %reduce-scatter.13.cloned.1.call-done = f32[64,512]{1,0:T(8,128)} async-done(((f32[1024,512]{1,0:T(8,128)}), f32[64,512]{1,0:T(8,128)}) %reduce-scatter.13.cloned.1.call-update) | async-done | bytes 131088
  630.9 177.8 %reduce-scatter.11.cloned.1.call-done = f32[64,2048]{1,0:T(8,128)} async-done(((f32[1024,2048]{1,0:T(8,128)}), f32[64,2048]{1,0:T(8,128)}) %reduce-scatter.11.cloned.1.call-update) | async-done | bytes 524304 | tf_op jit(solution)/shard_map/reduce_scatter | solution.py:137
  (67 shorter events, 40.8 us)
Async XLA Ops:
  7.2 8.6 %copy-start = (bf16[1024,1024]{1,0:T(8,128)(2,1)S(1)}, bf16[1024,1024]{1,0:T(8,128)(2,1)}, u32[]{:S(2)}) copy-start(bf16[1024,1024]{1,0:T(8,128)(2,1)} %param.7) | copy-start | bytes 6291460
  7.2 61.6 %all-gather.9.cloned.1.call-start = ((), (), s32[]{:S(2)}) async-start(), calls=%async_computation.6 | async-start | bytes 1114112 | tf_op jit(solution)/shard_map/all_gather | solution.py:38
  7.9 117.7 %all-gather.5.cloned.1.call-start = ((), (), s32[]{:S(2)}) async-start(), calls=%async_computation.4 | async-start | bytes 1114112 | tf_op jit(solution)/shard_map/all_gather | solution.py:39
  8.7 173.9 %all-gather.7.cloned.1.call-start = ((), (), s32[]{:S(2)}) async-start(), calls=%async_computation.5 | async-start | bytes 1114112 | tf_op jit(solution)/shard_map/all_gather | solution.py:40
  9.4 250.7 %all-gather.11.cloned.1.call-start = ((), (), s32[]{:S(2)}) async-start(), calls=%async_computation.7 | async-start | bytes 4456448 | tf_op jit(solution)/shard_map/all_gather | solution.py:41
  10.0 272.1 %all-reduce.4.cloned.1.call-start = ((), (), s32[]{:S(2)}) async-start(), calls=%async_computation.8 | async-start | bytes 917504 | tf_op jit(solution)/shard_map/psum | solution.py:94
  14.9 1.6 copy-start.6
  16.6 168.2 %copy-start.2 = (bf16[280,1024]{1,0:T(8,128)(2,1)}, bf16[280,1024]{1,0:T(8,128)(2,1)S(1)}, u32[]{:S(2)}) copy-start(bf16[280,1024]{1,0:T(8,128)(2,1)S(1)} %fusion.26) | copy-start | bytes 1720324
  70.7 194.1 %copy-start.3 = (bf16[280,512]{0,1:T(8,128)(2,1)}, bf16[280,512]{0,1:T(8,128)(2,1)S(1)}, u32[]{:S(2)}) copy-start(bf16[280,512]{0,1:T(8,128)(2,1)S(1)} %copy.23) | copy-start | bytes 860164
  264.8 136.3 %all-reduce.6.cloned.1.call-start = ((), (), s32[]{:S(2)}) async-start(), calls=%async_computation.9 | async-start | bytes 4194304 | tf_op jit(solution)/shard_map/psum | solution.py:132
  283.1 6.1 collective-permute-start.1
  291.3 5.9 copy-start.4
  291.3 6.6 copy-start.7
  361.5 108.0 %reduce-scatter.9.cloned.1.call-start = ((), (), s32[]{:S(2)}) async-start(), calls=%async_computation.10 | async-start | bytes 2228224 | tf_op jit(solution)/shard_map/reduce_scatter | solution.py:134
  364.8 185.4 %reduce-scatter.15.cloned.1.call-start = ((), (), s32[]{:S(2)}) async-start(), calls=%async_computation.13 | async-start | bytes 2228224
  374.3 3.0 copy-start.5
  374.3 256.5 %reduce-scatter.13.cloned.1.call-start = ((), (), s32[]{:S(2)}) async-start(), calls=%async_computation.12 | async-start | bytes 2228224
  377.3 431.3 %reduce-scatter.11.cloned.1.call-start = ((), (), s32[]{:S(2)}) async-start(), calls=%async_computation.11 | async-start | bytes 8912896 | tf_op jit(solution)/shard_map/reduce_scatter | solution.py:137
  377.4 15.0 %copy-start.1 = (bf16[224,2048]{1,0:T(8,128)(2,1)S(1)}, bf16[224,2048]{1,0:T(8,128)(2,1)}, u32[]{:S(2)}) copy-start(bf16[224,2048]{1,0:T(8,128)(2,1)} %param.13) | copy-start | bytes 2752516
  383.3 6.6 collective-permute-start
Sparse Core Ops, SparseCore 0:
  10.8 57.9 all-gather.8
  71.5 54.0 all-gather.4
  128.4 54.0 all-gather.6
  185.1 74.8 all-gather.10
  264.9 17.1 all-reduce.3
  361.6 23.2 all-reduce.5
  387.8 81.7 reduce-scatter.8
  472.4 77.8 reduce-scatter.14
  553.1 77.6 reduce-scatter.12
  633.6 174.9 reduce-scatter.10
where the time goes:
time: 821 us; the launch traced here: 819 us
  waiting for transfers between devices  655 us (80%)
  matrix products  113 us (14%)
  local copies, waits for them, and re-layouts  20.5 us (2%)
  between operations  16.3 us (2%)
    reduce_scatter x1, waiting for transfers between devices, local(): lax.psum_scatter(grad_out, 'seq', scatter_dimension=0, tiled=True)  178 us
    unnamed x12, waiting for transfers between devices  164 us
    all_gather x1, waiting for transfers between devices, local(): lax.all_gather(w_out, 'seq', axis=0, tiled=True)  70.1 us
    reduce_scatter x1, waiting for transfers between devices, local(): lax.psum_scatter(grad_query, 'seq', scatter_dimension=0, tiled=True)  68.4 us
    all_gather x1, waiting for transfers between devices, local(): lax.all_gather(w_key, 'seq', axis=0, tiled=True)  54.9 us
    all_gather x1, waiting for transfers between devices, local(): lax.all_gather(w_value, 'seq', axis=0, tiled=True)  54.6 us
    all_gather x1, waiting for transfers between devices, local(): lax.all_gather(w_query, 'seq', axis=0, tiled=True)  52.2 us
    dot_general x1, matrix products, local(): jnp.einsum('hsb,shd->bhd', score_grad, query_heads, preferred_element_typ...  25 us
  transfers between devices with their start and end apart: 12, of which 11 were waited for; matrix products, arithmetic and copies ran while one was open for 7% of the time, Pallas kernels for 0%

commit v1 on v0

v1 whole, which is shorter than its diff:
```python
import jax
import jax.numpy as jnp
from jax import lax
from jax.experimental import pallas as pl
from jax.experimental.pallas import tpu as pltpu
from jax.sharding import PartitionSpec as P

HEAD = 64
DRIFT = 56
MAXLEN = 16
SCALE = HEAD ** (-0.5)
VMEM_LIMIT = 48 * 1024 * 1024


def passed_along(value, axis, steps):
    count = lax.axis_size(axis)
    initial, last = (max(0, -steps), min(count, count - steps))
    return lax.ppermute(value, axis, [(source, source + steps) for source in range(initial, last)])


def swapped(value, axis, bit):
    count = lax.axis_size(axis)
    return lax.ppermute(value, axis, [(i, i ^ (1 << bit)) for i in range(count)])


def contract_cols(left_side, right_side):
    return lax.dot_general(
        left_side, right_side, (((1,), (1,)), ((), ())), preferred_element_type=jnp.float32
    )


def contract_rows(left_side, right_side):
    return lax.dot_general(
        left_side, right_side, (((0,), (0,)), ((), ())), preferred_element_type=jnp.float32
    )


def bit_order(axis, flip):
    bits = lax.axis_size(axis).bit_length() - 1
    order = list(range(bits))
    if flip and bits > 1:
        order[0], order[1] = 1, 0
    return order


def scatter_sum(value, axis, flip):
    count = lax.axis_size(axis)
    rank = lax.axis_index(axis)
    order = bit_order(axis, flip)
    bits = len(order)
    value = value.reshape((2,) * bits + (value.shape[0] // count, value.shape[1]))
    left = list(range(bits - 1, -1, -1))
    for bit in order:
        at = left.index(bit)
        mine = (rank >> bit) & 1
        send = lax.dynamic_index_in_dim(value, 1 - mine, at, keepdims=False)
        keep = lax.dynamic_index_in_dim(value, mine, at, keepdims=False)
        value = keep + swapped(send, axis, bit)
        left.pop(at)
    return value


def gather_rows(value, axis, flip):
    rank = lax.axis_index(axis)
    cols = value.shape[1]
    held = []
    for bit in reversed(bit_order(axis, flip)):
        other = swapped(value, axis, bit)
        mine = ((rank >> bit) & 1) == 0
        at = sum(1 for b in held if b > bit)
        value = jnp.stack([jnp.where(mine, value, other), jnp.where(mine, other, value)], axis=at)
        held.append(bit)
    return value.reshape(-1, cols)


def pair_sum(value, axis):
    if lax.axis_size(axis) != 2:
        return lax.psum(value, axis)
    other = swapped(value, axis, 0)
    return (value.astype(jnp.float32) + other.astype(jnp.float32)).astype(value.dtype)


def split_halves(product):
    high = product.astype(jnp.bfloat16)
    low = (product - high.astype(jnp.float32)).astype(jnp.bfloat16)
    return high, low


def neighbours(ids):
    pairs = []
    count = ids.shape[1]
    where_at = lax.broadcasted_iota(jnp.int32, ids.shape, 1)
    step = 1
    while step < MAXLEN:
        before = (pltpu.roll(ids, step, 1) == ids) & (where_at >= step)
        after = (pltpu.roll(ids, count - step, 1) == ids) & (where_at < count - step)
        pairs.append((step, before, after))
        step *= 2
    return pairs


def over_patch(value, pairs, combine, neutral):
    count = value.shape[1]
    ahead = behind = value
    for step, before, after in pairs:
        ahead = combine(ahead, jnp.where(before, pltpu.roll(ahead, step, 1), neutral))
        behind = combine(behind, jnp.where(after, pltpu.roll(behind, count - step, 1), neutral))
    return ahead, behind


def head_rows(heads, width):
    row = lax.broadcasted_iota(jnp.int32, (heads, width), 0)
    col = lax.broadcasted_iota(jnp.int32, (heads, width), 1)
    return ((col >= row * HEAD) & (col < row * HEAD + HEAD)).astype(jnp.float32).astype(jnp.bfloat16)


def forward_kernel(ids_ref, member_ref, query_ref, key_ref, value_ref, prob_ref, attended_ref):
    heads, width = prob_ref.shape[0], query_ref.shape[1]
    member = member_ref[...]
    expand = head_rows(heads, width)
    query_bytes = contract_rows(member, query_ref[...])
    high, low = split_halves(query_bytes * key_ref[...].astype(jnp.float32))
    scores = (contract_cols(expand, high) + contract_cols(expand, low)) * SCALE
    pairs = neighbours(jnp.broadcast_to(ids_ref[...], scores.shape))
    peak = jnp.maximum(*over_patch(scores, pairs, jnp.maximum, -1e30))
    terms = jnp.exp(scores - peak)
    ahead, behind = over_patch(terms, pairs, jnp.add, 0.0)
    prob = terms / (ahead + (behind - terms))
    prob_ref[...] = prob
    weight = contract_rows(prob.astype(jnp.bfloat16), expand)
    high, low = split_halves(weight * value_ref[...].astype(jnp.float32))
    attended = jnp.dot(member, high, preferred_element_type=jnp.float32) + jnp.dot(
        member, low, preferred_element_type=jnp.float32
    )
    attended_ref[...] = attended.astype(jnp.bfloat16)


def backward_kernel(
    ids_ref, member_ref, query_ref, key_ref, value_ref, prob_ref, grad_ref,
    key_grad_ref, value_grad_ref, query_grad_ref,
):
    heads, width = prob_ref.shape[0], query_ref.shape[1]
    member = member_ref[...]
    expand = head_rows(heads, width)
    prob = prob_ref[...]
    grad_bytes = contract_rows(member, grad_ref[...])
    high, low = split_halves(grad_bytes * value_ref[...].astype(jnp.float32))
    prob_grad = contract_cols(expand, high) + contract_cols(expand, low)
    value_weight = contract_rows(prob.astype(jnp.bfloat16), expand)
    value_grad_ref[...] = (value_weight * grad_bytes).astype(jnp.bfloat16)
    pairs = neighbours(jnp.broadcast_to(ids_ref[...], prob.shape))
    both = prob * prob_grad
    ahead, behind = over_patch(both, pairs, jnp.add, 0.0)
    score_grad = prob * (prob_grad - (ahead + (behind - both))) * SCALE
    weight = contract_rows(score_grad.astype(jnp.bfloat16), expand)
    query_bytes = contract_rows(member, query_ref[...])
    key_grad_ref[...] = (weight * query_bytes).astype(jnp.bfloat16)
    high, low = split_halves(weight * key_ref[...].astype(jnp.float32))
    query_grad = jnp.dot(member, high, preferred_element_type=jnp.float32) + jnp.dot(
        member, low, preferred_element_type=jnp.float32
    )
    query_grad_ref[...] = query_grad.astype(jnp.bfloat16)


def run_kernel(body, outs, *operands):
    vmem = pl.BlockSpec(memory_space=pltpu.VMEM)
    return pl.pallas_call(
        body,
        out_shape=outs,
        in_specs=[vmem] * len(operands),
        out_specs=[vmem] * len(outs),
        compiler_params=pltpu.CompilerParams(vmem_limit_bytes=VMEM_LIMIT),
        cost_estimate=pl.CostEstimate(
            flops=8_000_000_000, bytes_accessed=8_000_000, transcendentals=0
        ),
    )(*operands)


def local(byte_state, patch_id, w_query, w_key, w_value, w_out, out_grad):
    seq_rank = lax.axis_index("seq")
    model_rank = lax.axis_index("mp")
    n_model = lax.axis_size("mp")
    width = w_query.shape[1]
    half = width // 2
    heads = width // HEAD
    patch_rows = out_grad.shape[0]
    byte_rows = byte_state.shape[0]
    slots = -(-(patch_rows + DRIFT) // 128) * 128

    full_out = lax.all_gather(w_out, "seq", axis=0, tiled=True)
    first = gather_rows(jnp.concatenate([w_key, w_query[:, :half]], axis=1), "seq", False)
    second = gather_rows(jnp.concatenate([w_value, w_query[:, half:]], axis=1), "seq", True)
    full_key, full_value = first[:, :width], second[:, :width]
    full_query = jnp.concatenate([first[:, width:], second[:, width:]], axis=1)

    first_patch = patch_id[0]
    last_patch = patch_id[byte_rows - 1]
    slot_index = jnp.arange(slots, dtype=jnp.int32)
    ids = (patch_id - first_patch)[None, :]
    member = ids == slot_index[:, None]
    member_half = member.astype(jnp.bfloat16)
    length = jnp.maximum(jnp.sum(member.astype(jnp.float32), axis=1), 1.0)
    pooled = (
        jnp.dot(member_half, byte_state, preferred_element_type=jnp.float32) / length[:, None]
    ).astype(jnp.bfloat16)

    keys = jnp.dot(byte_state, full_key, preferred_element_type=jnp.float32).astype(jnp.bfloat16)
    values = jnp.dot(byte_state, full_value, preferred_element_type=jnp.float32).astype(
        jnp.bfloat16
    )
    query_proj = jnp.dot(pooled, full_query, preferred_element_type=jnp.float32).astype(
        jnp.bfloat16
    )
    prob, attended = run_kernel(
        forward_kernel,
        [
            jax.ShapeDtypeStruct((heads, byte_rows), jnp.float32),
            jax.ShapeDtypeStruct((slots, width), jnp.bfloat16),
        ],
        ids, member_half, query_proj, keys, values,
    )

    target_row = first_patch - seq_rank * patch_rows + slot_index
    slot_live = slot_index <= last_patch - first_patch
    own_map = (
        (target_row[None, :] == jnp.arange(patch_rows, dtype=jnp.int32)[:, None])
        & slot_live[None, :]
    ).astype(jnp.bfloat16)
    next_map = (
        (target_row[None, :] - patch_rows == jnp.arange(DRIFT, dtype=jnp.int32)[:, None])
        & slot_live[None, :]
    ).astype(jnp.bfloat16)
    outgoing = jnp.dot(next_map, attended, preferred_element_type=jnp.float32).astype(jnp.bfloat16)
    incoming = passed_along(outgoing, "seq", 1)
    own_block = jnp.dot(own_map, attended, preferred_element_type=jnp.float32)
    own_block = (
        own_block + jnp.pad(incoming.astype(jnp.float32), ((0, patch_rows - DRIFT), (0, 0)))
    ).astype(jnp.bfloat16)
    if n_model == 2:
        other_block = swapped(own_block, "mp", 0)
        heads_all = jnp.concatenate(
            [
                jnp.where(model_rank == 0, own_block, other_block),
                jnp.where(model_rank == 0, other_block, own_block),
            ],
            axis=1,
        )
    else:
        heads_all = lax.all_gather(own_block, "mp", axis=1, tiled=True)
    grad_out = contract_rows(heads_all, out_grad)
    out_half = grad_out.shape[1] // 2
    grad_out = jnp.concatenate(
        [
            scatter_sum(grad_out[:, :out_half], "seq", False),
            scatter_sum(grad_out[:, out_half:], "seq", True),
        ],
        axis=1,
    )
    patch_embed = jnp.dot(heads_all, full_out, preferred_element_type=jnp.float32).astype(
        jnp.bfloat16
    )

    partial_sum = contract_cols(out_grad, full_out).astype(jnp.bfloat16)
    if n_model == 2:
        mine = lax.dynamic_slice_in_dim(partial_sum, model_rank * width, width, 1)
        theirs = lax.dynamic_slice_in_dim(partial_sum, (1 - model_rank) * width, width, 1)
        head_grad = (
            mine.astype(jnp.float32) + swapped(theirs, "mp", 0).astype(jnp.float32)
        ).astype(jnp.bfloat16)
    else:
        head_grad = lax.dynamic_slice_in_dim(
            lax.psum(partial_sum, "mp"), model_rank * width, width, 1
        )
    returned = passed_along(head_grad[:DRIFT], "seq", -1)
    slot_grad = (contract_rows(own_map, head_grad) + contract_rows(next_map, returned)).astype(
        jnp.bfloat16
    )
    key_grad, value_grad, query_grad = run_kernel(
        backward_kernel,
        [
            jax.ShapeDtypeStruct((byte_rows, width), jnp.bfloat16),
            jax.ShapeDtypeStruct((byte_rows, width), jnp.bfloat16),
            jax.ShapeDtypeStruct((slots, width), jnp.bfloat16),
        ],
        ids, member_half, query_proj, keys, values, prob, slot_grad,
    )
    grad_key = scatter_sum(contract_rows(byte_state, key_grad), "seq", False)
    grad_value = scatter_sum(contract_rows(byte_state, value_grad), "seq", True)
    grad_query = contract_rows(pooled, query_grad)
    grad_query = jnp.concatenate(
        [
            scatter_sum(grad_query[:, :half], "seq", False),
            scatter_sum(grad_query[:, half:], "seq", True),
        ],
        axis=1,
    )
    pooled_grad = (contract_cols(query_grad, full_query) / length[:, None]).astype(jnp.bfloat16)
    byte_part = (
        contract_cols(key_grad, full_key)
        + contract_cols(value_grad, full_value)
        + contract_rows(member_half, pooled_grad)
    )
    byte_grad = pair_sum(byte_part.astype(jnp.bfloat16), "mp")
    return (patch_embed, byte_grad, grad_query, grad_key, grad_value, grad_out)


def solution(mesh):
    in_specs = (
        P("seq", None),
        P("seq"),
        P("seq", "mp"),
        P("seq", "mp"),
        P("seq", "mp"),
        P("seq", "mp"),
        P("seq", "mp"),
    )
    out_specs = (
        P("seq", "mp"),
        P("seq", None),
        P("seq", "mp"),
        P("seq", "mp"),
        P("seq", "mp"),
        P("seq", "mp"),
    )
    return jax.shard_map(local, mesh=mesh, in_specs=in_specs, out_specs=out_specs, check_vma=False)
```

time: 821 us -> 364 us (0.44)
  waiting for transfers between devices: 655 us -> 191 us
  matrix products: 113 us -> 34.3 us
  starting transfers between devices: 6.88 us -> 51.4 us
  other arithmetic: 4.69 us -> 29.2 us
  local copies, waits for them, and re-layouts: 20.5 us -> 32.3 us
    reduce_scatter x2 -> x0, waiting for transfers between devices: 246 us -> none  [the longest x1 178 us: local(): lax.psum_scatter(grad_out, 'seq', scatter_dimension=0, tiled=True)]
    all_gather x4 -> x1, waiting for transfers between devices: 232 us -> 0.02 us  [local(): full_out = lax.all_gather(w_out, 'seq', axis=0, tiled=True)]
    ppermute x0 -> x35, waiting for transfers between devices: none -> 186 us  [swapped(): return lax.ppermute(value, axis, [(i, i ^ 1 << bit) for i in range(count)])]
    unnamed x12 -> x1, waiting for transfers between devices: 164 us -> 0.68 us
    dot_general x6 -> x2, matrix products: 66.7 us -> 2.5 us  [the longest x1 1.25 us: local(): jnp.dot(byte_state, full_key, preferred_element_type=jnp.float32)]
    ppermute x0 -> x35, starting transfers between devices: none -> 46.1 us  [swapped(): return lax.ppermute(value, axis, [(i, i ^ 1 << bit) for i in range(count)])]
    add x0 -> x24, other arithmetic: none -> 15.6 us  [scatter_sum(): value = keep + swapped(send, axis, bit)]
    sub x1 -> x0, matrix products: 9.48 us -> none  [local(): exp_terms = jnp.where(member[None], jnp.exp(masked - peak), 0.0)]
  transfers between devices with their start and end apart: 12 -> 38, of which waited for: 11 -> 27; matrix products, arithmetic and copies ran while one was open for 7% -> 19% of each run, Pallas kernels for 0% -> 1%
where the time goes in v1:
time: 364 us; the launch traced here: 362 us
  waiting for transfers between devices  191 us (52%)
  starting transfers between devices  51.4 us (14%)
  matrix products  34.3 us (9%)
  local copies, waits for them, and re-layouts  32.3 us (9%)
  other arithmetic  29.2 us (8%)
  between operations  17 us (5%)
  Pallas kernels  7.17 us (2%)
    ppermute x35, waiting for transfers between devices, swapped(): return lax.ppermute(value, axis, [(i, i ^ 1 << bit) for i in range(count)])  186 us
    ppermute x35, starting transfers between devices, swapped(): return lax.ppermute(value, axis, [(i, i ^ 1 << bit) for i in range(count)])  46.1 us
    add x24, other arithmetic, scatter_sum(): value = keep + swapped(send, axis, bit)  15.6 us
    dot_general x7, matrix products, contract_rows(): lax.dot_general(left_side, right_side, (((0,), (0,)), ((), ())), preferre...  15.6 us
    dot_general x3, matrix products, contract_cols(): lax.dot_general(left_side, right_side, (((1,), (1,)), ((), ())), preferre...  12.2 us
  transfers between devices with their start and end apart: 38, of which 27 were waited for; matrix products, arithmetic and copies ran while one was open for 19% of the time, Pallas kernels for 1%

profile of v1, /device:TPU:0, one launch (start us, length us, event | category | flops | bytes accessed | tf_op | source)
XLA Modules:
  0.0 362.5 jit_solution(17528354909311081598)
XLA Ops:
  9.6 4.0 %collective-permute-start.4 = (bf16[64,768]{1,0:T(8,128)(2,1)S(1)}, bf16[64,768]{1,0:T(8,128)(2,1)}, u32[]{:S(2)}, u32[]{:S(2)}) collective-permute-start(bf16[64,768]{1,0:T(8,128)(2,1)S(1)} %pad_maximum_fusion.18), channel_id=1, source_target_pairs={{0,16},{2,18},{4,20},{6,22},{8,24},{10,26},{12,28},{14,30},{16,0},... | collective-permute-start | bytes 294920 | tf_op jit(solution)/shard_map/ppermute | solution.py:23
  27.3 7.0 %collective-permute-done.1 = bf16[2,64,768]{2,1,0:T(8,128)(2,1)S(1)} collective-permute-done((bf16[2,64,768]{2,1,0:T(8,128)(2,1)S(1)}, bf16[2,64,768]{2,1,0:T(8,128)(2,1)S(1)}, u32[]{:S(2)}, u32[]{:S(2)}) %collective-permute-start.1) | collective-permute-done | bytes 196640 | tf_op jit(solution)/shard_map/ppermute | solution.py:23
  41.8 6.3 %collective-permute-done.2 = bf16[2,2,64,768]{3,2,1,0:T(8,128)(2,1)} collective-permute-done((bf16[2,2,64,768]{3,2,1,0:T(8,128)(2,1)}, bf16[2,2,64,768]{3,2,1,0:T(8,128)(2,1)}, u32[]{:S(2)}, u32[]{:S(2)}) %collective-permute-start.2) | collective-permute-done | bytes 393248 | tf_op jit(solution)/shard_map/ppermute | solution.py:23
  53.0 6.7 %collective-permute-done.6 = bf16[2,2,64,768]{3,2,0,1:T(8,128)(2,1)S(1)} collective-permute-done((bf16[2,2,64,768]{3,2,0,1:T(8,128)(2,1)S(1)}, bf16[2,2,64,768]{3,2,0,1:T(8,128)(2,1)S(1)}, u32[]{:S(2)}, u32[]{:S(2)}) %collective-permute-start.6) | collective-permute-done | bytes 393248 | tf_op jit(solution)/shard_map/ppermute | solution.py:23
  61.3 18.1 %collective-permute-done.3 = bf16[2,2,2,64,768]{4,3,2,1,0:T(8,128)(2,1)S(1)} collective-permute-done((bf16[2,2,2,64,768]{4,3,2,1,0:T(8,128)(2,1)S(1)}, bf16[2,2,2,64,768]{4,3,2,1,0:T(8,128)(2,1)S(1)}, u32[]{:S(2)}, u32[]{:S(2)}) %collective-permute-start.3) | collective-permute-done | bytes 786464 | tf_op jit(solution)/shard_map/ppermute | solution.py:23
  81.0 3.8 %collective-permute-done.7 = bf16[2,2,2,64,768]{4,3,0,1,2:T(8,128)(2,1)S(1)} collective-permute-done((bf16[2,2,2,64,768]{4,3,0,1,2:T(8,128)(2,1)S(1)}, bf16[2,2,2,64,768]{4,3,0,1,2:T(8,128)(2,1)S(1)}, u32[]{:S(2)}, u32[]{:S(2)}) %collective-permute-start.7) | collective-permute-done | bytes 786464 | tf_op jit(solution)/shard_map/ppermute | solution.py:23
  88.3 3.4 shard_map.118
  91.9 3.8 %collective-permute-start.8 = (bf16[56,512]{1,0:T(8,128)(2,1)S(1)}, bf16[56,512]{1,0:T(8,128)(2,1)S(1)}, u32[]{:S(2)}, u32[]{:S(2)}) collective-permute-start(bf16[56,512]{1,0:T(8,128)(2,1)S(1)} %convolution_convert_fusion.5), channel_id=1, source_target_pairs={{0,2},{2,4},{4,6},{6,8},{8,10},{10,12},{12,14},{14,16},{16,18},{18... | collective-permute-start | bytes 172040 | tf_op jit(solution)/shard_map/ppermute | solution.py:18
  101.7 3.3 fusion.38
  108.2 4.1 %collective-permute-start.33 = (f32[2,2,2,64,1024]{4,3,1,0,2:T(8,128)}, f32[2,2,2,64,1024]{4,3,1,0,2:T(8,128)}, u32[]{:S(2)}, u32[]{:S(2)}) collective-permute-start(f32[2,2,2,64,1024]{4,3,1,0,2:T(8,128)} %bitcast.174), channel_id=1, source_target_pairs={{0,4},{2,6},{4,0},{6,2},{8,12},{10,14},{12,8},{14,10},{16,20},{18,... | collective-permute-start | bytes 6291464 | tf_op jit(solution)/shard_map/ppermute | solution.py:23
  115.8 42.8 %collective-permute-done.33 = f32[2,2,2,64,1024]{4,3,1,0,2:T(8,128)} collective-permute-done((f32[2,2,2,64,1024]{4,3,1,0,2:T(8,128)}, f32[2,2,2,64,1024]{4,3,1,0,2:T(8,128)}, u32[]{:S(2)}, u32[]{:S(2)}) %collective-permute-start.33) | collective-permute-done | bytes 2097184 | tf_op jit(solution)/shard_map/ppermute | solution.py:23
  165.3 20.2 %collective-permute-done.34 = f32[2,2,64,1024]{3,2,1,0:T(8,128)} collective-permute-done((f32[2,2,64,1024]{3,2,1,0:T(8,128)S(1)}, f32[2,2,64,1024]{3,2,1,0:T(8,128)}, u32[]{:S(2)}, u32[]{:S(2)}) %collective-permute-start.34) | collective-permute-done | bytes 1048608 | tf_op jit(solution)/shard_map/ppermute | solution.py:23
  194.0 9.3 %collective-permute-done.35 = f32[2,64,1024]{2,1,0:T(8,128)} collective-permute-done((f32[2,64,1024]{2,1,0:T(8,128)}, f32[2,64,1024]{2,1,0:T(8,128)}, u32[]{:S(2)}, u32[]{:S(2)}) %collective-permute-start.35) | collective-permute-done | bytes 524320 | tf_op jit(solution)/shard_map/ppermute | solution.py:23
  207.3 10.5 %collective-permute-done.31 = f32[2,64,1024]{2,1,0:T(8,128)} collective-permute-done((f32[2,64,1024]{2,1,0:T(8,128)}, f32[2,64,1024]{2,1,0:T(8,128)}, u32[]{:S(2)}, u32[]{:S(2)}) %collective-permute-start.31) | collective-permute-done | bytes 524320 | tf_op jit(solution)/shard_map/ppermute | solution.py:23
  220.5 10.7 %collective-permute-done.32 = f32[64,1024]{1,0:T(8,128)} collective-permute-done((f32[64,1024]{1,0:T(8,128)S(1)}, f32[64,1024]{1,0:T(8,128)}, u32[]{:S(2)}, u32[]{:S(2)}) %collective-permute-start.32) | collective-permute-done | bytes 262176 | tf_op jit(solution)/shard_map/ppermute | solution.py:23
  232.2 4.0 %convolution_convert_fusion.3 = bf16[224,1024]{1,0:T(8,128)(2,1)S(1)} fusion(bf16[224,2048]{1,0:T(8,128)(2,1)} %param.13, bf16[1024,2048]{1,0:T(8,128)(2,1)} %all-gather.2.cloned.1.call-done), kind=kOutput, calls=%fused_computation.23 | convolution fusion | flops 939753472 | bytes 5570560 | tf_op jit(solution)/shard_map/dot_general | solution.py:27
  244.7 3.8 %shard_map.119 = (bf16[1024,512]{1,0:T(8,128)(2,1)S(1)}, bf16[1024,512]{1,0:T(8,128)(2,1)S(1)}, bf16[384,512]{1,0:T(8,128)(2,1)S(1)}) custom-call(s32[1,1024]{1,0:T(1,128)S(1)} %bitcast.179, bf16[384,1024]{1,0:T(8,128)(2,1)S(1)} %copy-done.2, bf16[384,512]{1,0:T(8,128)(2,1)S(1)} %copy-done.4, bf16[1024,512]{1,0:T(8,128)(2,1)S(1)} %copy-done.6, ...), custom_call_target="tpu_custom_call" | custom-call | flops 8000000000 | bytes 8000000 | tf_op jit(solution)/shard_map/pallas_call | solution.py:167
  251.2 3.3 fusion.8
  256.6 4.9 %fusion = f32[1024,1024]{1,0:T(8,128)} fusion(bf16[384,512]{1,0:T(8,128)(2,1)S(1)} %get-tuple-element.15, f32[384]{0:T(512)S(1)} %broadcast_maximum_fusion, s32[1024]{0:T(1024)S(1)} %broadcast_subtract_fusion, bf16[1024,256]{1,0:T(8,128)(2,1)} %copy-done.31, bf16[1024,256]{1,0:T(8,128)(2,1)} %copy-done.30), kind=kOutput, calls=%fused_computation.15 | convolution fusion | flops 1211236352 | bytes 5641728 | tf_op jit(solution)/shard_map/dot_general | solution.py:33
  283.2 4.8 %add_convert_fusion.1 = bf16[1024,1024]{1,0:T(8,128)(2,1)S(1)} fusion(f32[1024,1024]{1,0:T(8,128)} %fusion, f32[1024,1024]{1,0:T(8,128)} %fusion.8, bf16[1024,512]{1,0:T(8,128)(2,1)S(1)} %get-tuple-element.14, bf16[1024,768]{1,0:T(8,128)(2,1)S(1)} %bitcast.188), kind=kOutput, calls=%fused_computation.1 | convolution fusion | flops 1076887552 | bytes 12582912 | tf_op jit(solution)/shard_map/dot_general | solution.py:27
  294.4 15.6 %collective-permute-done.18 = f32[2,2,64,256]{3,2,1,0:T(8,128)S(1)} collective-permute-done((f32[2,2,64,256]{3,2,1,0:T(8,128)S(1)}, f32[2,2,64,256]{3,2,1,0:T(8,128)S(1)}, u32[]{:S(2)}, u32[]{:S(2)}) %collective-permute-start.18) | collective-permute-done | bytes 262176 | tf_op jit(solution)/shard_map/ppermute | solution.py:23
  326.0 6.9 %collective-permute-done.22 = f32[2,2,64,512]{3,2,1,0:T(8,128)S(1)} collective-permute-done((f32[2,2,64,512]{3,2,1,0:T(8,128)S(1)}, f32[2,2,64,512]{3,2,1,0:T(8,128)S(1)}, u32[]{:S(2)}, u32[]{:S(2)}) %collective-permute-start.22) | collective-permute-done | bytes 524320 | tf_op jit(solution)/shard_map/ppermute | solution.py:23
  335.6 5.8 %collective-permute-done.23 = f32[2,64,512]{2,1,0:T(8,128)S(1)} collective-permute-done((f32[2,64,512]{2,1,0:T(8,128)S(1)}, f32[2,64,512]{2,1,0:T(8,128)S(1)}, u32[]{:S(2)}, u32[]{:S(2)}) %collective-permute-start.23) | collective-permute-done | bytes 262176 | tf_op jit(solution)/shard_map/ppermute | solution.py:23
  348.1 4.6 %collective-permute-done.28 = f32[64,512]{1,0:T(8,128)S(1)} collective-permute-done((f32[64,512]{1,0:T(8,128)S(1)}, f32[64,512]{1,0:T(8,128)S(1)}, u32[]{:S(2)}, u32[]{:S(2)}) %collective-permute-start.28) | collective-permute-done | bytes 131104 | tf_op jit(solution)/shard_map/ppermute | solution.py:23
  (233 shorter events, 137.8 us)
Async XLA Ops:
  7.2 225.0 %all-gather.2.cloned.1.call-start = ((), (), s32[]{:S(2)}) async-start(), calls=%async_computation | async-start | bytes 4456448 | tf_op jit(solution)/shard_map/all_gather | solution.py:190
  9.6 14.9 %collective-permute-start.4 = (bf16[64,768]{1,0:T(8,128)(2,1)S(1)}, bf16[64,768]{1,0:T(8,128)(2,1)}, u32[]{:S(2)}, u32[]{:S(2)}) collective-permute-start(bf16[64,768]{1,0:T(8,128)(2,1)S(1)} %pad_maximum_fusion.18), channel_id=1, source_target_pairs={{0,16},{2,18},{4,20},{6,22},{8,24},{10,26},{12,28},{14,30},{16,0},... | collective-permute-start | bytes 294920 | tf_op jit(solution)/shard_map/ppermute | solution.py:23
  23.6 10.7 %collective-permute-start.1 = (bf16[2,64,768]{2,1,0:T(8,128)(2,1)S(1)}, bf16[2,64,768]{2,1,0:T(8,128)(2,1)S(1)}, u32[]{:S(2)}, u32[]{:S(2)}) collective-permute-start(bf16[2,64,768]{2,1,0:T(8,128)(2,1)S(1)} %pad_maximum_fusion.14), channel_id=1, source_target_pairs={{0,8},{2,10},{4,12},{6,14},{8,0},{10,2},{12,4},{14,6},{16,24},{18,... | collective-permute-start | bytes 589832 | tf_op jit(solution)/shard_map/ppermute | solution.py:23
  26.0 13.2 %collective-permute-start.5 = (bf16[2,64,768]{2,1,0:T(8,128)(2,1)}, bf16[2,64,768]{2,1,0:T(8,128)(2,1)}, u32[]{:S(2)}, u32[]{:S(2)}) collective-permute-start(bf16[2,64,768]{2,1,0:T(8,128)(2,1)} %pad_maximum_fusion.15), channel_id=1, source_target_pairs={{0,8},{2,10},{4,12},{6,14},{8,0},{10,2},{12,4},{14,6},{16,24},{18,... | collective-permute-start | bytes 589832 | tf_op jit(solution)/shard_map/ppermute | solution.py:23
  35.2 12.9 %collective-permute-start.2 = (bf16[2,2,64,768]{3,2,1,0:T(8,128)(2,1)}, bf16[2,2,64,768]{3,2,1,0:T(8,128)(2,1)}, u32[]{:S(2)}, u32[]{:S(2)}) collective-permute-start(bf16[2,2,64,768]{3,2,1,0:T(8,128)(2,1)} %pad_maximum_fusion.10), channel_id=1, source_target_pairs={{0,4},{2,6},{4,0},{6,2},{8,12},{10,14},{12,8},{14,10},{16,20},{18,... | collective-permute-start | bytes 1179656 | tf_op jit(solution)/shard_map/ppermute | solution.py:23
  40.3 19.4 %collective-permute-start.6 = (bf16[2,2,64,768]{3,2,0,1:T(8,128)(2,1)S(1)}, bf16[2,2,64,768]{3,2,0,1:T(8,128)(2,1)S(1)}, u32[]{:S(2)}, u32[]{:S(2)}) collective-permute-start(bf16[2,2,64,768]{3,2,0,1:T(8,128)(2,1)S(1)} %pad_maximum_fusion.11), channel_id=1, source_target_pairs={{0,2},{2,0},{4,6},{6,4},{8,10},{10,8},{12,14},{14,12},{16,18},{18,... | collective-permute-start | bytes 1179656 | tf_op jit(solution)/shard_map/ppermute | solution.py:23
  49.3 30.1 %collective-permute-start.3 = (bf16[2,2,2,64,768]{4,3,2,1,0:T(8,128)(2,1)S(1)}, bf16[2,2,2,64,768]{4,3,2,1,0:T(8,128)(2,1)S(1)}, u32[]{:S(2)}, u32[]{:S(2)}) collective-permute-start(bf16[2,2,2,64,768]{4,3,2,1,0:T(8,128)(2,1)S(1)} %pad_maximum_fusion.3), channel_id=1, source_target_pairs={{0,2},{2,0},{4,6},{6,4},{8,10},{10,8},{12,14},{14,12},{16,18},{18,... | collective-permute-start | bytes 2359304 | tf_op jit(solution)/shard_map/ppermute | solution.py:23
  59.8 25.0 %collective-permute-start.7 = (bf16[2,2,2,64,768]{4,3,0,1,2:T(8,128)(2,1)S(1)}, bf16[2,2,2,64,768]{4,3,0,1,2:T(8,128)(2,1)S(1)}, u32[]{:S(2)}, u32[]{:S(2)}) collective-permute-start(bf16[2,2,2,64,768]{4,3,0,1,2:T(8,128)(2,1)S(1)} %pad_maximum_fusion.4), channel_id=1, source_target_pairs={{0,4},{2,6},{4,0},{6,2},{8,12},{10,14},{12,8},{14,10},{16,20},{18,... | collective-permute-start | bytes 2359304 | tf_op jit(solution)/shard_map/ppermute | solution.py:23
  108.2 50.3 %collective-permute-start.33 = (f32[2,2,2,64,1024]{4,3,1,0,2:T(8,128)}, f32[2,2,2,64,1024]{4,3,1,0,2:T(8,128)}, u32[]{:S(2)}, u32[]{:S(2)}) collective-permute-start(f32[2,2,2,64,1024]{4,3,1,0,2:T(8,128)} %bitcast.174), channel_id=1, source_target_pairs={{0,4},{2,6},{4,0},{6,2},{8,12},{10,14},{12,8},{14,10},{16,20},{18,... | collective-permute-start | bytes 6291464 | tf_op jit(solution)/shard_map/ppermute | solution.py:23
  115.1 47.5 %collective-permute-start.29 = (f32[2,2,2,64,1024]{4,3,1,0,2:T(8,128)S(1)}, f32[2,2,2,64,1024]{4,3,1,0,2:T(8,128)S(1)}, u32[]{:S(2)}, u32[]{:S(2)}) collective-permute-start(f32[2,2,2,64,1024]{4,3,1,0,2:T(8,128)S(1)} %bitcast.194), channel_id=1, source_target_pairs={{0,2},{2,0},{4,6},{6,4},{8,10},{10,8},{12,14},{14,12},{16,18},{18,... | collective-permute-start | bytes 6291464 | tf_op jit(solution)/shard_map/ppermute | solution.py:23
  160.7 24.9 %collective-permute-start.34 = (f32[2,2,64,1024]{3,2,1,0:T(8,128)S(1)}, f32[2,2,64,1024]{3,2,1,0:T(8,128)}, u32[]{:S(2)}, u32[]{:S(2)}) collective-permute-start(f32[2,2,64,1024]{3,2,1,0:T(8,128)S(1)} %dynamic-slice_bitcast_fusion), channel_id=1, source_target_pairs={{0,2},{2,0},{4,6},{6,4},{8,10},{10,8},{12,14},{14,12},{16,18},{18,... | collective-permute-start | bytes 3145736 | tf_op jit(solution)/shard_map/ppermute | solution.py:23
  164.7 25.5 %collective-permute-start.30 = (f32[2,2,64,1024]{3,2,1,0:T(8,128)}, f32[2,2,64,1024]{3,2,1,0:T(8,128)}, u32[]{:S(2)}, u32[]{:S(2)}) collective-permute-start(f32[2,2,64,1024]{3,2,1,0:T(8,128)} %dynamic-slice_bitcast_fusion.1), channel_id=1, source_target_pairs={{0,4},{2,6},{4,0},{6,2},{8,12},{10,14},{12,8},{14,10},{16,20},{18,... | collective-permute-start | bytes 3145736 | tf_op jit(solution)/shard_map/ppermute | solution.py:23
  188.0 15.3 %collective-permute-start.35 = (f32[2,64,1024]{2,1,0:T(8,128)}, f32[2,64,1024]{2,1,0:T(8,128)}, u32[]{:S(2)}, u32[]{:S(2)}) collective-permute-start(f32[2,64,1024]{2,1,0:T(8,128)} %dynamic-slice_bitcast_fusion.4), channel_id=1, source_target_pairs={{0,8},{2,10},{4,12},{6,14},{8,0},{10,2},{12,4},{14,6},{16,24},{18,... | collective-permute-start | bytes 1572872 | tf_op jit(solution)/shard_map/ppermute | solution.py:23
  193.4 24.4 %collective-permute-start.31 = (f32[2,64,1024]{2,1,0:T(8,128)}, f32[2,64,1024]{2,1,0:T(8,128)}, u32[]{:S(2)}, u32[]{:S(2)}) collective-permute-start(f32[2,64,1024]{2,1,0:T(8,128)} %dynamic-slice_bitcast_fusion.5), channel_id=1, source_target_pairs={{0,8},{2,10},{4,12},{6,14},{8,0},{10,2},{12,4},{14,6},{16,24},{18,... | collective-permute-start | bytes 1572872 | tf_op jit(solution)/shard_map/ppermute | solution.py:23
  204.5 14.9 %collective-permute-start.36 = (f32[64,1024]{1,0:T(8,128)S(1)}, f32[64,1024]{1,0:T(8,128)}, u32[]{:S(2)}, u32[]{:S(2)}) collective-permute-start(f32[64,1024]{1,0:T(8,128)S(1)} %dynamic-slice_bitcast_fusion.8), channel_id=1, source_target_pairs={{0,16},{2,18},{4,20},{6,22},{8,24},{10,26},{12,28},{14,30},{16,0},... | collective-permute-start | bytes 786440 | tf_op jit(solution)/shard_map/ppermute | solution.py:23
  219.0 12.2 %collective-permute-start.32 = (f32[64,1024]{1,0:T(8,128)S(1)}, f32[64,1024]{1,0:T(8,128)}, u32[]{:S(2)}, u32[]{:S(2)}) collective-permute-start(f32[64,1024]{1,0:T(8,128)S(1)} %dynamic-slice_bitcast_fusion.9), channel_id=1, source_target_pairs={{0,16},{2,18},{4,20},{6,22},{8,24},{10,26},{12,28},{14,30},{16,0},... | collective-permute-start | bytes 786440 | tf_op jit(solution)/shard_map/ppermute | solution.py:23
  266.7 21.4 %collective-permute-start.17 = (f32[2,2,2,64,256]{4,3,1,0,2:T(8,128)}, f32[2,2,2,64,256]{4,3,1,0,2:T(8,128)}, u32[]{:S(2)}, u32[]{:S(2)}) collective-permute-start(f32[2,2,2,64,256]{4,3,1,0,2:T(8,128)} %bitcast.176), channel_id=1, source_target_pairs={{0,4},{2,6},{4,0},{6,2},{8,12},{10,14},{12,8},{14,10},{16,20},{18,... | collective-permute-start | bytes 1572872 | tf_op jit(solution)/shard_map/ppermute | solution.py:23
  268.3 23.1 %collective-permute-start.13 = (f32[2,2,2,64,256]{4,3,1,0,2:T(8,128)}, f32[2,2,2,64,256]{4,3,1,0,2:T(8,128)}, u32[]{:S(2)}, u32[]{:S(2)}) collective-permute-start(f32[2,2,2,64,256]{4,3,1,0,2:T(8,128)} %bitcast.177), channel_id=1, source_target_pairs={{0,2},{2,0},{4,6},{6,4},{8,10},{10,8},{12,14},{14,12},{16,18},{18,... | collective-permute-start | bytes 1572872 | tf_op jit(solution)/shard_map/ppermute | solution.py:23
  275.8 46.2 %collective-permute-start.21 = (f32[2,2,2,64,512]{4,3,2,1,0:T(8,128)}, f32[2,2,2,64,512]{4,3,2,1,0:T(8,128)}, u32[]{:S(2)}, u32[]{:S(2)}) collective-permute-start(f32[2,2,2,64,512]{4,3,2,1,0:T(8,128)} %dynamic-slice_bitcast_fusion.3), channel_id=1, source_target_pairs={{0,2},{2,0},{4,6},{6,4},{8,10},{10,8},{12,14},{14,12},{16,18},{18,... | collective-permute-start | bytes 3145736 | tf_op jit(solution)/shard_map/ppermute | solution.py:23
  282.9 41.5 %collective-permute-start.25 = (f32[2,2,2,64,512]{4,3,2,1,0:T(8,128)S(1)}, f32[2,2,2,64,512]{4,3,2,1,0:T(8,128)S(1)}, u32[]{:S(2)}, u32[]{:S(2)}) collective-permute-start(f32[2,2,2,64,512]{4,3,2,1,0:T(8,128)S(1)} %dynamic-slice_bitcast_fusion.2), channel_id=1, source_target_pairs={{0,4},{2,6},{4,0},{6,2},{8,12},{10,14},{12,8},{14,10},{16,20},{18,... | collective-permute-start | bytes 3145736 | tf_op jit(solution)/shard_map/ppermute | solution.py:23
  288.0 65.3 %collective-permute-start.12 = (bf16[1024,1024]{1,0:T(8,128)(2,1)S(1)}, bf16[1024,1024]{1,0:T(8,128)(2,1)S(1)}, u32[]{:S(2)}, u32[]{:S(2)}) collective-permute-start(bf16[1024,1024]{1,0:T(8,128)(2,1)S(1)} %add_convert_fusion.1), channel_id=1, source_target_pairs={{0,1},{1,0},{2,3},{3,2},{4,5},{5,4},{6,7},{7,6},{8,9},{9,8},{10,11... | collective-permute-start | bytes 6291464 | tf_op jit(solution)/shard_map/ppermute | solution.py:23
  289.3 20.7 %collective-permute-start.18 = (f32[2,2,64,256]{3,2,1,0:T(8,128)S(1)}, f32[2,2,64,256]{3,2,1,0:T(8,128)S(1)}, u32[]{:S(2)}, u32[]{:S(2)}) collective-permute-start(f32[2,2,64,256]{3,2,1,0:T(8,128)S(1)} %dynamic-slice_bitcast_fusion.12), channel_id=1, source_target_pairs={{0,2},{2,0},{4,6},{6,4},{8,10},{10,8},{12,14},{14,12},{16,18},{18,... | collective-permute-start | bytes 786440 | tf_op jit(solution)/shard_map/ppermute | solution.py:23
  292.5 19.9 %collective-permute-start.14 = (f32[2,2,64,256]{3,2,1,0:T(8,128)S(1)}, f32[2,2,64,256]{3,2,1,0:T(8,128)S(1)}, u32[]{:S(2)}, u32[]{:S(2)}) collective-permute-start(f32[2,2,64,256]{3,2,1,0:T(8,128)S(1)} %dynamic-slice_bitcast_fusion.13), channel_id=1, source_target_pairs={{0,4},{2,6},{4,0},{6,2},{8,12},{10,14},{12,8},{14,10},{16,20},{18,... | collective-permute-start | bytes 786440 | tf_op jit(solution)/shard_map/ppermute | solution.py:23
  334.8 10.5 %collective-permute-start.27 = (f32[2,64,512]{2,1,0:T(8,128)S(1)}, f32[2,64,512]{2,1,0:T(8,128)S(1)}, u32[]{:S(2)}, u32[]{:S(2)}) collective-permute-start(f32[2,64,512]{2,1,0:T(8,128)S(1)} %dynamic-slice_bitcast_fusion.10), channel_id=1, source_target_pairs={{0,8},{2,10},{4,12},{6,14},{8,0},{10,2},{12,4},{14,6},{16,24},{18,... | collective-permute-start | bytes 786440 | tf_op jit(solution)/shard_map/ppermute | solution.py:23
  (48 other events, 485.4 us)
Sparse Core Ops, SparseCore 0:
  10.8 92.1 all-gather.1

commit v2 on v1

--- a/solution.py
+++ b/solution.py
@@ -35,41 +35,83 @@
     )
 
 
-def bit_order(axis, flip):
+def bit_order(axis, flip, start=0):
     bits = lax.axis_size(axis).bit_length() - 1
-    order = list(range(bits))
-    if flip and bits > 1:
-        order[0], order[1] = 1, 0
+    order = list(range(start, bits))
+    if flip and len(order) > 1:
+        order[0], order[1] = order[1], order[0]
     return order
 
 
-def scatter_sum(value, axis, flip):
-    count = lax.axis_size(axis)
+def after(value, earlier):
+    return lax.optimization_barrier((value, earlier))[0]
+
+
+def scatter_sum(value, axis, flip, start=0):
     rank = lax.axis_index(axis)
-    order = bit_order(axis, flip)
+    order = bit_order(axis, flip, start)
     bits = len(order)
-    value = value.reshape((2,) * bits + (value.shape[0] // count, value.shape[1]))
-    left = list(range(bits - 1, -1, -1))
+    value = value.reshape((2,) * bits + (value.shape[0] >> bits, value.shape[1]))
+    left = sorted(order, reverse=True)
     for bit in order:
         at = left.index(bit)
         mine = (rank >> bit) & 1
         send = lax.dynamic_index_in_dim(value, 1 - mine, at, keepdims=False)
         keep = lax.dynamic_index_in_dim(value, mine, at, keepdims=False)
-        value = keep + swapped(send, axis, bit)
+        other = swapped(send, axis, bit)
+        value = keep + other
         left.pop(at)
     return value
 
 
-def gather_rows(value, axis, flip):
+def gather_rows(value, axis, flip, order=None):
     rank = lax.axis_index(axis)
     cols = value.shape[1]
     held = []
-    for bit in reversed(bit_order(axis, flip)):
+    for bit in reversed(bit_order(axis, flip)) if order is None else order:
         other = swapped(value, axis, bit)
         mine = ((rank >> bit) & 1) == 0
         at = sum(1 for b in held if b > bit)
         value = jnp.stack([jnp.where(mine, value, other), jnp.where(mine, other, value)], axis=at)
         held.append(bit)
+    return value.reshape(-1, cols)
+
+
+def gather_pair(value, axis, held, bit):
+    rank = lax.axis_index(axis)
+    other = swapped(value, axis, bit)
+    mine = ((rank >> bit) & 1) == 0
+    at = 1 if held > bit else 0
+    value = jnp.stack([jnp.where(mine, value, other), jnp.where(mine, other, value)], axis=at)
+    return value.reshape(-1, value.shape[-1])
+
+
+def grouped_columns(value, axis, group):
+    width = value.shape[1]
+    count = lax.axis_size(axis)
+    block = width // count
+    source = lax.broadcasted_iota(jnp.int32, (width, width), 0)
+    place = lax.broadcasted_iota(jnp.int32, (width, width), 1)
+    owner = (place % (width >> group)) // block << group
+    for bit in range(group):
+        owner = owner + ((place // (width >> (bit + 1))) % 2 << bit)
+    chosen = (source == owner * block + place % block).astype(jnp.bfloat16)
+    return jnp.dot(value, chosen, preferred_element_type=jnp.float32).astype(value.dtype)
+
+
+def grouped_rows(value, axis, group):
+    rank = lax.axis_index(axis)
+    cols = value.shape[1]
+    value = value[None]
+    for bit in range(group):
+        cols //= 2
+        upper = ((rank >> bit) & 1) == 1
+        low, high = value[:, :, :cols], value[:, :, cols:]
+        keep, send = jnp.where(upper, high, low), jnp.where(upper, low, high)
+        other = swapped(send, axis, bit)
+        value = jnp.concatenate(
+            [jnp.where(upper, other, keep), jnp.where(upper, keep, other)], axis=0
+        )
     return value.reshape(-1, cols)
 
 
@@ -187,11 +229,28 @@
     byte_rows = byte_state.shape[0]
     slots = -(-(patch_rows + DRIFT) // 128) * 128
 
-    full_out = lax.all_gather(w_out, "seq", axis=0, tiled=True)
     first = gather_rows(jnp.concatenate([w_key, w_query[:, :half]], axis=1), "seq", False)
     second = gather_rows(jnp.concatenate([w_value, w_query[:, half:]], axis=1), "seq", True)
     full_key, full_value = first[:, :width], second[:, :width]
     full_query = jnp.concatenate([first[:, width:], second[:, width:]], axis=1)
+
+    group = min(2, lax.axis_size("seq").bit_length() - 1)
+    out_half = w_out.shape[1] // 2
+    full_out = jnp.concatenate(
+        [
+            gather_rows(after(w_out[:, :out_half], first), "seq", False),
+            gather_rows(after(w_out[:, out_half:], second), "seq", True),
+        ],
+        axis=1,
+    )
+    steps = [list(range(group)), list(range(group))[::-1]]
+    part = [after(out_grad[:, :out_half], full_out), after(out_grad[:, out_half:], full_out)]
+    part = [gather_rows(p, "seq", False, s[:1]) for p, s in zip(part, steps)]
+    shared = [
+        gather_pair(p.reshape(2, patch_rows, out_half), "seq", s[0], s[1]) if group == 2 else p
+        for p, s in zip(part, steps)
+    ]
+    group_out_grad = jnp.concatenate(shared, axis=1)
 
     first_patch = patch_id[0]
     last_patch = patch_id[byte_rows - 1]
@@ -247,15 +306,8 @@
         )
     else:
         heads_all = lax.all_gather(own_block, "mp", axis=1, tiled=True)
-    grad_out = contract_rows(heads_all, out_grad)
-    out_half = grad_out.shape[1] // 2
-    grad_out = jnp.concatenate(
-        [
-            scatter_sum(grad_out[:, :out_half], "seq", False),
-            scatter_sum(grad_out[:, out_half:], "seq", True),
-        ],
-        axis=1,
-    )
+    group_heads = grouped_rows(grouped_columns(heads_all, "seq", group), "seq", group)
+    grad_out = contract_rows(group_heads, group_out_grad)
     patch_embed = jnp.dot(heads_all, full_out, preferred_element_type=jnp.float32).astype(
         jnp.bfloat16
     )
@@ -282,7 +334,14 @@
             jax.ShapeDtypeStruct((byte_rows, width), jnp.bfloat16),
             jax.ShapeDtypeStruct((slots, width), jnp.bfloat16),
         ],
-        ids, member_half, query_proj, keys, values, prob, slot_grad,
+        ids, member_half, query_proj, keys, values, prob, after(slot_grad, part),
+    )
+    grad_out = jnp.concatenate(
+        [
+            scatter_sum(grad_out[:, :out_half], "seq", False, group),
+            scatter_sum(grad_out[:, out_half:], "seq", True, group),
+        ],
+        axis=1,
     )
     grad_key = scatter_sum(contract_rows(byte_state, key_grad), "seq", False)
     grad_value = scatter_sum(contract_rows(byte_state, value_grad), "seq", True)

time: 364 us -> 332 us (0.912)
  between operations: 17 us -> 3.59 us
  starting transfers between devices: 51.4 us -> 64.5 us
  local copies, waits for them, and re-layouts: 32.3 us -> 20 us
  waiting for transfers between devices: 191 us -> 183 us
  other arithmetic: 29.2 us -> 23 us
  matrix products: 34.3 us -> 30.3 us
    ppermute x35 -> x45, starting transfers between devices: 46.1 us -> 59.4 us  [swapped(): return lax.ppermute(value, axis, [(i, i ^ 1 << bit) for i in range(count)])]
    add x24 -> x21, other arithmetic: 15.6 us -> 3.92 us  [the longest x20 3.91 us: scatter_sum(): value = keep + other]
    dynamic_slice x4 -> x2, local copies, waits for them, and re-layouts: 6.06 us -> 0.16 us  [scatter_sum(): keep = lax.dynamic_index_in_dim(value, mine, at, keepdims=False)]
    ppermute x2, waiting for transfers between devices: 4.07 us -> 0.01 us  [passed_along(): lax.ppermute(value, axis, [(source, source + steps) for source in range(i...]
    another operation x16 -> x35, other arithmetic: 6.18 us -> 10.1 us  [gather_rows(): jnp.stack([jnp.where(mine, value, other), jnp.where(mine, other, value)],...]
    dot_general x3, matrix products: 12.2 us -> 8.31 us  [contract_cols(): lax.dot_general(left_side, right_side, (((1,), (1,)), ((), ())), preferre...]
    ppermute x35 -> x45, waiting for transfers between devices: 186 us -> 183 us  [swapped(): return lax.ppermute(value, axis, [(i, i ^ 1 << bit) for i in range(count)])]
  transfers between devices with their start and end apart: 38 -> 47, of which waited for: 27 -> 25; matrix products, arithmetic and copies ran while one was open for 19% -> 18% of each run, Pallas kernels for 1% -> 1%
where the time goes in v2:
time: 332 us
  waiting for transfers between devices  183 us (55%)
  starting transfers between devices  64.5 us (19%)
  matrix products  30.3 us (9%)
  other arithmetic  23 us (7%)
  local copies, waits for them, and re-layouts  20 us (6%)
  Pallas kernels  7.16 us (2%)
  between operations  3.59 us (1%)
    ppermute x45, waiting for transfers between devices, swapped(): return lax.ppermute(value, axis, [(i, i ^ 1 << bit) for i in range(count)])  183 us
    ppermute x45, starting transfers between devices, swapped(): return lax.ppermute(value, axis, [(i, i ^ 1 << bit) for i in range(count)])  59.4 us
    dot_general x7, matrix products, contract_rows(): lax.dot_general(left_side, right_side, (((0,), (0,)), ((), ())), preferre...  14.2 us
    another operation x35, other arithmetic, gather_rows(): jnp.stack([jnp.where(mine, value, other), jnp.where(mine, other, value)],...  10.1 us
    dot_general x3, matrix products, contract_cols(): lax.dot_general(left_side, right_side, (((1,), (1,)), ((), ())), preferre...  8.31 us
    pallas_call x2, Pallas kernels, run_kernel(): pl.pallas_call(body, out_shape=outs, in_specs=[vmem] * len(operands), out...  7.16 us
  transfers between devices with their start and end apart: 47, of which 25 were waited for; matrix products, arithmetic and copies ran while one was open for 18% of the time, Pallas kernels for 1%

profile of v2, /device:TPU:0, one launch (start us, length us, event | category | flops | bytes accessed | tf_op | source)
XLA Modules:
  0.0 331.7 jit_solution(16699672747295120119)
XLA Ops:
  2.5 4.0 %collective-permute-start = (bf16[64,768]{1,0:T(8,128)(2,1)S(1)}, bf16[64,768]{1,0:T(8,128)(2,1)S(1)}, u32[]{:S(2)}, u32[]{:S(2)}) collective-permute-start(bf16[64,768]{1,0:T(8,128)(2,1)S(1)} %pad_maximum_fusion.32), channel_id=1, source_target_pairs={{0,16},{2,18},{4,20},{6,22},{8,24},{10,26},{12,28},{14,30},{16,0},... | collective-permute-start | bytes 294920 | tf_op jit(solution)/shard_map/ppermute | solution.py:23
  19.0 3.6 %collective-permute-done.1 = bf16[2,64,768]{2,1,0:T(8,128)(2,1)S(1)} collective-permute-done((bf16[2,64,768]{2,1,0:T(8,128)(2,1)S(1)}, bf16[2,64,768]{2,1,0:T(8,128)(2,1)S(1)}, u32[]{:S(2)}, u32[]{:S(2)}) %collective-permute-start.1) | collective-permute-done | bytes 196640 | tf_op jit(solution)/shard_map/ppermute | solution.py:23
  28.5 3.8 %collective-permute-done.2 = bf16[2,2,64,768]{3,2,1,0:T(8,128)(2,1)} collective-permute-done((bf16[2,2,64,768]{3,2,1,0:T(8,128)(2,1)}, bf16[2,2,64,768]{3,2,1,0:T(8,128)(2,1)}, u32[]{:S(2)}, u32[]{:S(2)}) %collective-permute-start.2) | collective-permute-done | bytes 393248 | tf_op jit(solution)/shard_map/ppermute | solution.py:23
  35.9 3.2 collective-permute-done.6
  40.8 13.2 %collective-permute-done.3 = bf16[2,2,2,64,768]{4,3,2,1,0:T(8,128)(2,1)S(1)} collective-permute-done((bf16[2,2,2,64,768]{4,3,2,1,0:T(8,128)(2,1)S(1)}, bf16[2,2,2,64,768]{4,3,2,1,0:T(8,128)(2,1)S(1)}, u32[]{:S(2)}, u32[]{:S(2)}) %collective-permute-start.3) | collective-permute-done | bytes 786464 | tf_op jit(solution)/shard_map/ppermute | solution.py:23
  59.1 3.3 %shard_map.118 = (f32[8,1024]{1,0:T(8,128)S(1)}, bf16[384,512]{1,0:T(8,128)(2,1)S(1)}) custom-call(s32[1,1024]{1,0:T(1,128)S(1)} %bitcast.227, bf16[384,1024]{1,0:T(8,128)(2,1)S(1)} %fusion.42.member_ref, bf16[384,512]{1,0:T(8,128)(2,1)S(1)} %convolution_convert_fusion.4.query_ref, bf16[1024,512]{1,0:T(8,128)(2,1)S(1)} %fusion.43.key_ref, ...), custom_call_target="tpu_custom_call" | custom-call | flops 8000000000 | bytes 8000000 | tf_op jit(solution)/shard_map/pallas_call | solution.py:209
  62.6 3.6 %collective-permute-start.8 = (bf16[56,512]{1,0:T(8,128)(2,1)S(1)}, bf16[56,512]{1,0:T(8,128)(2,1)S(1)}, u32[]{:S(2)}, u32[]{:S(2)}) collective-permute-start(bf16[56,512]{1,0:T(8,128)(2,1)S(1)} %convolution_convert_fusion.5), channel_id=1, source_target_pairs={{0,2},{2,4},{4,6},{6,8},{8,10},{10,12},{12,14},{14,16},{16,18},{18... | collective-permute-start | bytes 172040 | tf_op jit(solution)/shard_map/ppermute | solution.py:18
  69.6 7.5 %collective-permute-done.10 = bf16[64,1024]{1,0:T(8,128)(2,1)S(1)} collective-permute-done((bf16[64,1024]{1,0:T(8,128)(2,1)S(1)}, bf16[64,1024]{1,0:T(8,128)(2,1)S(1)}, u32[]{:S(2)}, u32[]{:S(2)}) %collective-permute-start.10) | collective-permute-done | bytes 131104 | tf_op jit(solution)/shard_map/ppermute | solution.py:23
  83.8 8.0 %collective-permute-done.15 = bf16[2,64,1024]{2,1,0:T(8,128)(2,1)S(1)} collective-permute-done((bf16[2,64,1024]{2,1,0:T(8,128)(2,1)S(1)}, bf16[2,64,1024]{2,1,0:T(8,128)(2,1)S(1)}, u32[]{:S(2)}, u32[]{:S(2)}) %collective-permute-start.15) | collective-permute-done | bytes 262176 | tf_op jit(solution)/shard_map/ppermute | solution.py:23
  94.5 9.3 %collective-permute-done.16 = bf16[2,2,64,1024]{3,2,0,1:T(8,128)(2,1)S(1)} collective-permute-done((bf16[2,2,64,1024]{3,2,0,1:T(8,128)(2,1)S(1)}, bf16[2,2,64,1024]{3,2,0,1:T(8,128)(2,1)S(1)}, u32[]{:S(2)}, u32[]{:S(2)}) %collective-permute-start.16) | collective-permute-done | bytes 524320 | tf_op jit(solution)/shard_map/ppermute | solution.py:23
  109.0 23.6 %collective-permute-done.38 = bf16[2,224,256]{2,1,0:T(8,128)(2,1)S(1)} collective-permute-done((bf16[2,224,256]{2,1,0:T(8,128)(2,1)S(1)}, bf16[2,224,256]{2,1,0:T(8,128)(2,1)S(1)}, u32[]{:S(2)}, u32[]{:S(2)}) %collective-permute-start.38) | collective-permute-done | bytes 229408 | tf_op jit(solution)/shard_map/ppermute | solution.py:23
  144.9 3.8 %shard_map.119 = (bf16[1024,512]{1,0:T(8,128)(2,1)S(1)}, bf16[1024,512]{1,0:T(8,128)(2,1)S(1)}, bf16[384,512]{1,0:T(8,128)(2,1)S(1)}) custom-call(s32[1,1024]{1,0:T(1,128)S(1)} %bitcast.228, bf16[384,1024]{1,0:T(8,128)(2,1)S(1)} %copy-done.2, bf16[384,512]{1,0:T(8,128)(2,1)S(1)} %convolution_convert_fusion.4.query_ref, ...), custom_call_target="tpu_custom_call" | custom-call | flops 8000000000 | bytes 8000000 | tf_op jit(solution)/shard_map/pallas_call | solution.py:209
  151.4 3.3 %fusion.54 = f32[1024,1024]{1,0:T(8,128)} fusion(bf16[1024,512]{1,0:T(8,128)(2,1)S(1)} %get-tuple-element.19, bf16[1024,768]{1,0:T(8,128)(2,1)S(1)} %bitcast.244), kind=kOutput, calls=%fused_computation.99 | convolution fusion | flops 1073741824 | bytes 6291456 | tf_op jit(solution)/shard_map/dot_general | solution.py:27
  156.8 4.9 %fusion.40 = f32[1024,1024]{1,0:T(8,128)} fusion(bf16[384,512]{1,0:T(8,128)(2,1)S(1)} %get-tuple-element.21, f32[384]{0:T(512)S(1)} %broadcast_maximum_fusion, s32[1024]{0:T(1024)S(1)} %broadcast_subtract_fusion, bf16[1024,256]{1,0:T(8,128)(2,1)} %copy-done.11, bf16[1024,256]{1,0:T(8,128)(2,1)} %copy-done.10), kind=kOutput, calls=%fused_computation.72 | convolution fusion | flops 1211236352 | bytes 5641728 | tf_op jit(solution)/shard_map/dot_general | solution.py:33
  180.0 3.5 %add_convert_fusion.1 = bf16[1024,1024]{1,0:T(8,128)(2,1)S(1)} fusion(f32[1024,1024]{1,0:T(8,128)} %fusion.40, f32[1024,1024]{1,0:T(8,128)S(1)} %copy-done.8, bf16[1024,512]{1,0:T(8,128)(2,1)S(1)} %get-tuple-element.20, bf16[1024,768]{1,0:T(8,128)(2,1)S(1)} %bitcast.235), kind=kOutput, calls=%fused_computation.33 | convolution fusion | flops 1076887552 | bytes 12582912 | tf_op jit(solution)/shard_map/dot_general | solution.py:27
  186.9 24.1 %collective-permute-done.21 = f32[2,2,2,64,256]{4,3,1,0,2:T(8,128)S(1)} collective-permute-done((f32[2,2,2,64,256]{4,3,1,0,2:T(8,128)S(1)}, f32[2,2,2,64,256]{4,3,1,0,2:T(8,128)S(1)}, u32[]{:S(2)}, u32[]{:S(2)}) %collective-permute-start.21) | collective-permute-done | bytes 524320 | tf_op jit(solution)/shard_map/ppermute | solution.py:23
  213.3 23.6 %collective-permute-done.22 = f32[2,2,64,256]{3,2,1,0:T(8,128)S(1)} collective-permute-done((f32[2,2,64,256]{3,2,1,0:T(8,128)S(1)}, f32[2,2,64,256]{3,2,1,0:T(8,128)S(1)}, u32[]{:S(2)}, u32[]{:S(2)}) %collective-permute-start.22) | collective-permute-done | bytes 262176 | tf_op jit(solution)/shard_map/ppermute | solution.py:23
  238.0 5.3 %collective-permute-done.26 = f32[2,2,64,256]{3,2,1,0:T(8,128)S(1)} collective-permute-done((f32[2,2,64,256]{3,2,1,0:T(8,128)S(1)}, f32[2,2,64,256]{3,2,1,0:T(8,128)S(1)}, u32[]{:S(2)}, u32[]{:S(2)}) %collective-permute-start.26) | collective-permute-done | bytes 262176 | tf_op jit(solution)/shard_map/ppermute | solution.py:23
  244.9 4.0 %collective-permute-done.23 = f32[2,64,256]{2,1,0:T(8,128)S(1)} collective-permute-done((f32[2,64,256]{2,1,0:T(8,128)S(1)}, f32[2,64,256]{2,1,0:T(8,128)S(1)}, u32[]{:S(2)}, u32[]{:S(2)}) %collective-permute-start.23) | collective-permute-done | bytes 131104 | tf_op jit(solution)/shard_map/ppermute | solution.py:23
  250.4 3.4 %collective-permute-done.27 = f32[2,64,256]{2,1,0:T(8,128)S(1)} collective-permute-done((f32[2,64,256]{2,1,0:T(8,128)S(1)}, f32[2,64,256]{2,1,0:T(8,128)S(1)}, u32[]{:S(2)}, u32[]{:S(2)}) %collective-permute-start.27) | collective-permute-done | bytes 131104 | tf_op jit(solution)/shard_map/ppermute | solution.py:23
  255.6 3.3 %collective-permute-done.24 = f32[64,256]{1,0:T(8,128)S(1)} collective-permute-done((f32[64,256]{1,0:T(8,128)S(1)}, f32[64,256]{1,0:T(8,128)S(1)}, u32[]{:S(2)}, u32[]{:S(2)}) %collective-permute-start.24) | collective-permute-done | bytes 65568 | tf_op jit(solution)/shard_map/ppermute | solution.py:23
  260.8 3.4 %collective-permute-done.28 = f32[64,256]{1,0:T(8,128)S(1)} collective-permute-done((f32[64,256]{1,0:T(8,128)S(1)}, f32[64,256]{1,0:T(8,128)S(1)}, u32[]{:S(2)}, u32[]{:S(2)}) %collective-permute-start.28) | collective-permute-done | bytes 65568 | tf_op jit(solution)/shard_map/ppermute | solution.py:23
  270.8 13.3 %collective-permute-done.42 = bf16[2,224,1024]{2,1,0:T(8,128)(2,1)S(1)} collective-permute-done((bf16[2,224,1024]{2,1,0:T(8,128)(2,1)S(1)}, bf16[2,224,1024]{2,1,0:T(8,128)(2,1)S(1)}, u32[]{:S(2)}, u32[]{:S(2)}) %collective-permute-start.42) | collective-permute-done | bytes 917536 | tf_op jit(solution)/shard_map/ppermute | solution.py:23
  293.4 16.7 %collective-permute-done.43 = f32[2,64,1024]{2,1,0:T(8,128)S(1)} collective-permute-done((f32[2,64,1024]{2,1,0:T(8,128)S(1)}, f32[2,64,1024]{2,1,0:T(8,128)S(1)}, u32[]{:S(2)}, u32[]{:S(2)}) %collective-permute-start.43) | collective-permute-done | bytes 524320 | tf_op jit(solution)/shard_map/ppermute | solution.py:23
  (242 shorter events, 132.2 us)
Async XLA Ops:
  33.5 20.5 %collective-permute-start.3 = (bf16[2,2,2,64,768]{4,3,2,1,0:T(8,128)(2,1)S(1)}, bf16[2,2,2,64,768]{4,3,2,1,0:T(8,128)(2,1)S(1)}, u32[]{:S(2)}, u32[]{:S(2)}) collective-permute-start(bf16[2,2,2,64,768]{4,3,2,1,0:T(8,128)(2,1)S(1)} %pad_maximum_fusion.12), channel_id=1, source_target_pairs={{0,2},{2,0},{4,6},{6,4},{8,10},{10,8},{12,14},{14,12},{16,18},{18,... | collective-permute-start | bytes 2359304 | tf_op jit(solution)/shard_map/ppermute | solution.py:23
  39.2 16.4 %collective-permute-start.7 = (bf16[2,2,2,64,768]{4,3,0,1,2:T(8,128)(2,1)S(1)}, bf16[2,2,2,64,768]{4,3,0,1,2:T(8,128)(2,1)S(1)}, u32[]{:S(2)}, u32[]{:S(2)}) collective-permute-start(bf16[2,2,2,64,768]{4,3,0,1,2:T(8,128)(2,1)S(1)} %pad_maximum_fusion.13), channel_id=1, source_target_pairs={{0,4},{2,6},{4,0},{6,2},{8,12},{10,14},{12,8},{14,10},{16,20},{18,... | collective-permute-start | bytes 2359304 | tf_op jit(solution)/shard_map/ppermute | solution.py:23
  78.9 14.5 %collective-permute-start.11 = (bf16[2,64,1024]{2,1,0:T(8,128)(2,1)S(1)}, bf16[2,64,1024]{2,1,0:T(8,128)(2,1)S(1)}, u32[]{:S(2)}, u32[]{:S(2)}) collective-permute-start(bf16[2,64,1024]{2,1,0:T(8,128)(2,1)S(1)} %pad_maximum_fusion.26), channel_id=1, source_target_pairs={{0,8},{2,10},{4,12},{6,14},{8,0},{10,2},{12,4},{14,6},{16,24},{18,... | collective-permute-start | bytes 786440 | tf_op jit(solution)/shard_map/ppermute | solution.py:23
  79.0 12.8 %collective-permute-start.15 = (bf16[2,64,1024]{2,1,0:T(8,128)(2,1)S(1)}, bf16[2,64,1024]{2,1,0:T(8,128)(2,1)S(1)}, u32[]{:S(2)}, u32[]{:S(2)}) collective-permute-start(bf16[2,64,1024]{2,1,0:T(8,128)(2,1)S(1)} %pad_maximum_fusion.27), channel_id=1, source_target_pairs={{0,8},{2,10},{4,12},{6,14},{8,0},{10,2},{12,4},{14,6},{16,24},{18,... | collective-permute-start | bytes 786440 | tf_op jit(solution)/shard_map/ppermute | solution.py:23
  93.6 13.0 %collective-permute-start.12 = (bf16[2,2,64,1024]{3,2,1,0:T(8,128)(2,1)S(1)}, bf16[2,2,64,1024]{3,2,1,0:T(8,128)(2,1)S(1)}, u32[]{:S(2)}, u32[]{:S(2)}) collective-permute-start(bf16[2,2,64,1024]{3,2,1,0:T(8,128)(2,1)S(1)} %pad_maximum_fusion.17), channel_id=1, source_target_pairs={{0,4},{2,6},{4,0},{6,2},{8,12},{10,14},{12,8},{14,10},{16,20},{18,... | collective-permute-start | bytes 1572872 | tf_op jit(solution)/shard_map/ppermute | solution.py:23
  104.0 29.5 %collective-permute-start.17 = (bf16[2,2,2,64,1024]{4,3,0,1,2:T(8,128)(2,1)S(1)}, bf16[2,2,2,64,1024]{4,3,0,1,2:T(8,128)(2,1)S(1)}, u32[]{:S(2)}, u32[]{:S(2)}) collective-permute-start(bf16[2,2,2,64,1024]{4,3,0,1,2:T(8,128)(2,1)S(1)} %pad_maximum_fusion.9), channel_id=1, source_target_pairs={{0,4},{2,6},{4,0},{6,2},{8,12},{10,14},{12,8},{14,10},{16,20},{18,... | collective-permute-start | bytes 3145736 | tf_op jit(solution)/shard_map/ppermute | solution.py:23
  105.7 26.9 %collective-permute-start.38 = (bf16[2,224,256]{2,1,0:T(8,128)(2,1)S(1)}, bf16[2,224,256]{2,1,0:T(8,128)(2,1)S(1)}, u32[]{:S(2)}, u32[]{:S(2)}) collective-permute-start(bf16[2,224,256]{2,1,0:T(8,128)(2,1)S(1)} %broadcast_select_fusion.7), channel_id=1, source_target_pairs={{0,4},{2,6},{4,0},{6,2},{8,12},{10,14},{12,8},{14,10},{16,20},{18,... | collective-permute-start | bytes 688136 | tf_op jit(solution)/shard_map/ppermute | solution.py:23
  106.7 27.3 %collective-permute-start.13 = (bf16[2,2,2,64,1024]{4,3,2,1,0:T(8,128)(2,1)S(1)}, bf16[2,2,2,64,1024]{4,3,2,1,0:T(8,128)(2,1)S(1)}, u32[]{:S(2)}, u32[]{:S(2)}) collective-permute-start(bf16[2,2,2,64,1024]{4,3,2,1,0:T(8,128)(2,1)S(1)} %pad_maximum_fusion.8), channel_id=1, source_target_pairs={{0,2},{2,0},{4,6},{6,4},{8,10},{10,8},{12,14},{14,12},{16,18},{18,... | collective-permute-start | bytes 3145736 | tf_op jit(solution)/shard_map/ppermute | solution.py:23
  141.2 42.6 %collective-permute-start.39 = (bf16[224,1024]{1,0:T(8,128)(2,1)}, bf16[224,1024]{1,0:T(8,128)(2,1)}, u32[]{:S(2)}, u32[]{:S(2)}) collective-permute-start(bf16[224,1024]{1,0:T(8,128)(2,1)} %get-tuple-element.22), channel_id=1, source_target_pairs={{0,2},{2,0},{4,6},{6,4},{8,10},{10,8},{12,14},{14,12},{16,18},{18,... | collective-permute-start | bytes 1376264 | tf_op jit(solution)/shard_map/ppermute | solution.py:23
  143.8 41.6 %collective-permute-start.41 = (bf16[224,1024]{1,0:T(8,128)(2,1)}, bf16[224,1024]{1,0:T(8,128)(2,1)}, u32[]{:S(2)}, u32[]{:S(2)}) collective-permute-start(bf16[224,1024]{1,0:T(8,128)(2,1)} %get-tuple-element.23), channel_id=1, source_target_pairs={{0,4},{2,6},{4,0},{6,2},{8,12},{10,14},{12,8},{14,10},{16,20},{18,... | collective-permute-start | bytes 1376264 | tf_op jit(solution)/shard_map/ppermute | solution.py:23
  169.6 96.6 %collective-permute-start.33 = (f32[2,2,2,64,512]{4,3,2,1,0:T(8,128)}, f32[2,2,2,64,512]{4,3,2,1,0:T(8,128)}, u32[]{:S(2)}, u32[]{:S(2)}) collective-permute-start(f32[2,2,2,64,512]{4,3,2,1,0:T(8,128)} %dynamic-slice_bitcast_fusion), channel_id=1, source_target_pairs={{0,4},{2,6},{4,0},{6,2},{8,12},{10,14},{12,8},{14,10},{16,20},{18,... | collective-permute-start | bytes 3145736 | tf_op jit(solution)/shard_map/ppermute | solution.py:23
  175.6 93.0 %collective-permute-start.29 = (f32[2,2,2,64,512]{4,3,2,1,0:T(8,128)S(1)}, f32[2,2,2,64,512]{4,3,2,1,0:T(8,128)S(1)}, u32[]{:S(2)}, u32[]{:S(2)}) collective-permute-start(f32[2,2,2,64,512]{4,3,2,1,0:T(8,128)S(1)} %dynamic-slice_bitcast_fusion.1), channel_id=1, source_target_pairs={{0,2},{2,0},{4,6},{6,4},{8,10},{10,8},{12,14},{14,12},{16,18},{18,... | collective-permute-start | bytes 3145736 | tf_op jit(solution)/shard_map/ppermute | solution.py:23
  177.6 33.4 %collective-permute-start.21 = (f32[2,2,2,64,256]{4,3,1,0,2:T(8,128)S(1)}, f32[2,2,2,64,256]{4,3,1,0,2:T(8,128)S(1)}, u32[]{:S(2)}, u32[]{:S(2)}) collective-permute-start(f32[2,2,2,64,256]{4,3,1,0,2:T(8,128)S(1)} %bitcast.251), channel_id=1, source_target_pairs={{0,2},{2,0},{4,6},{6,4},{8,10},{10,8},{12,14},{14,12},{16,18},{18,... | collective-permute-start | bytes 1572872 | tf_op jit(solution)/shard_map/ppermute | solution.py:23
  183.7 27.8 %collective-permute-start.25 = (f32[2,2,2,64,256]{4,3,1,0,2:T(8,128)S(1)}, f32[2,2,2,64,256]{4,3,1,0,2:T(8,128)S(1)}, u32[]{:S(2)}, u32[]{:S(2)}) collective-permute-start(f32[2,2,2,64,256]{4,3,1,0,2:T(8,128)S(1)} %bitcast.252), channel_id=1, source_target_pairs={{0,4},{2,6},{4,0},{6,2},{8,12},{10,14},{12,8},{14,10},{16,20},{18,... | collective-permute-start | bytes 1572872 | tf_op jit(solution)/shard_map/ppermute | solution.py:23
  185.4 144.0 %collective-permute-start.20 = (bf16[1024,1024]{1,0:T(8,128)(2,1)S(1)}, bf16[1024,1024]{1,0:T(8,128)(2,1)S(1)}, u32[]{:S(2)}, u32[]{:S(2)}) collective-permute-start(bf16[1024,1024]{1,0:T(8,128)(2,1)S(1)} %add_convert_fusion.1), channel_id=1, source_target_pairs={{0,1},{1,0},{2,3},{3,2},{4,5},{5,4},{6,7},{7,6},{8,9},{9,8},{10,11... | collective-permute-start | bytes 6291464 | tf_op jit(solution)/shard_map/ppermute | solution.py:23
  211.0 59.5 %collective-permute-start.40 = (bf16[2,224,1024]{2,1,0:T(8,128)(2,1)S(1)}, bf16[2,224,1024]{2,1,0:T(8,128)(2,1)S(1)}, u32[]{:S(2)}, u32[]{:S(2)}) collective-permute-start(bf16[2,224,1024]{2,1,0:T(8,128)(2,1)S(1)} %pad_maximum_fusion.10), channel_id=1, source_target_pairs={{0,4},{2,6},{4,0},{6,2},{8,12},{10,14},{12,8},{14,10},{16,20},{18,... | collective-permute-start | bytes 2752520 | tf_op jit(solution)/shard_map/ppermute | solution.py:23
  211.6 25.4 %collective-permute-start.22 = (f32[2,2,64,256]{3,2,1,0:T(8,128)S(1)}, f32[2,2,64,256]{3,2,1,0:T(8,128)S(1)}, u32[]{:S(2)}, u32[]{:S(2)}) collective-permute-start(f32[2,2,64,256]{3,2,1,0:T(8,128)S(1)} %dynamic-slice_bitcast_fusion.11), channel_id=1, source_target_pairs={{0,4},{2,6},{4,0},{6,2},{8,12},{10,14},{12,8},{14,10},{16,20},{18,... | collective-permute-start | bytes 786440 | tf_op jit(solution)/shard_map/ppermute | solution.py:23
  264.1 19.9 %collective-permute-start.42 = (bf16[2,224,1024]{2,1,0:T(8,128)(2,1)S(1)}, bf16[2,224,1024]{2,1,0:T(8,128)(2,1)S(1)}, u32[]{:S(2)}, u32[]{:S(2)}) collective-permute-start(bf16[2,224,1024]{2,1,0:T(8,128)(2,1)S(1)} %pad_maximum_fusion.11), channel_id=1, source_target_pairs={{0,2},{2,0},{4,6},{6,4},{8,10},{10,8},{12,14},{14,12},{16,18},{18,... | collective-permute-start | bytes 2752520 | tf_op jit(solution)/shard_map/ppermute | solution.py:23
  267.8 23.1 %collective-permute-start.34 = (f32[2,2,64,512]{3,2,1,0:T(8,128)S(1)}, f32[2,2,64,512]{3,2,1,0:T(8,128)S(1)}, u32[]{:S(2)}, u32[]{:S(2)}) collective-permute-start(f32[2,2,64,512]{3,2,1,0:T(8,128)S(1)} %dynamic-slice_bitcast_fusion.4), channel_id=1, source_target_pairs={{0,2},{2,0},{4,6},{6,4},{8,10},{10,8},{12,14},{14,12},{16,18},{18,... | collective-permute-start | bytes 1572872 | tf_op jit(solution)/shard_map/ppermute | solution.py:23
  268.9 22.5 %collective-permute-start.30 = (f32[2,2,64,512]{3,2,1,0:T(8,128)S(1)}, f32[2,2,64,512]{3,2,1,0:T(8,128)S(1)}, u32[]{:S(2)}, u32[]{:S(2)}) collective-permute-start(f32[2,2,64,512]{3,2,1,0:T(8,128)S(1)} %dynamic-slice_bitcast_fusion.5), channel_id=1, source_target_pairs={{0,4},{2,6},{4,0},{6,2},{8,12},{10,14},{12,8},{14,10},{16,20},{18,... | collective-permute-start | bytes 1572872 | tf_op jit(solution)/shard_map/ppermute | solution.py:23
  286.8 23.3 %collective-permute-start.43 = (f32[2,64,1024]{2,1,0:T(8,128)S(1)}, f32[2,64,1024]{2,1,0:T(8,128)S(1)}, u32[]{:S(2)}, u32[]{:S(2)}) collective-permute-start(f32[2,64,1024]{2,1,0:T(8,128)S(1)} %dynamic-slice_bitcast_fusion.3), channel_id=1, source_target_pairs={{0,8},{2,10},{4,12},{6,14},{8,0},{10,2},{12,4},{14,6},{16,24},{18,... | collective-permute-start | bytes 1572872 | tf_op jit(solution)/shard_map/ppermute | solution.py:23
  288.4 23.5 %collective-permute-start.45 = (f32[2,64,1024]{2,1,0:T(8,128)S(1)}, f32[2,64,1024]{2,1,0:T(8,128)S(1)}, u32[]{:S(2)}, u32[]{:S(2)}) collective-permute-start(f32[2,64,1024]{2,1,0:T(8,128)S(1)} %dynamic-slice_bitcast_fusion.2), channel_id=1, source_target_pairs={{0,16},{2,18},{4,20},{6,22},{8,24},{10,26},{12,28},{14,30},{16,0},... | collective-permute-start | bytes 1572872 | tf_op jit(solution)/shard_map/ppermute | solution.py:23
  291.1 23.4 %collective-permute-start.35 = (f32[2,64,512]{2,1,0:T(8,128)S(1)}, f32[2,64,512]{2,1,0:T(8,128)S(1)}, u32[]{:S(2)}, u32[]{:S(2)}) collective-permute-start(f32[2,64,512]{2,1,0:T(8,128)S(1)} %dynamic-slice_bitcast_fusion.8), channel_id=1, source_target_pairs={{0,8},{2,10},{4,12},{6,14},{8,0},{10,2},{12,4},{14,6},{16,24},{18,... | collective-permute-start | bytes 786440 | tf_op jit(solution)/shard_map/ppermute | solution.py:23
  291.5 28.4 %collective-permute-start.31 = (f32[2,64,512]{2,1,0:T(8,128)S(1)}, f32[2,64,512]{2,1,0:T(8,128)S(1)}, u32[]{:S(2)}, u32[]{:S(2)}) collective-permute-start(f32[2,64,512]{2,1,0:T(8,128)S(1)} %dynamic-slice_bitcast_fusion.9), channel_id=1, source_target_pairs={{0,8},{2,10},{4,12},{6,14},{8,0},{10,2},{12,4},{14,6},{16,24},{18,... | collective-permute-start | bytes 786440 | tf_op jit(solution)/shard_map/ppermute | solution.py:23
  (39 other events, 390.9 us)

commit v3 on v2

--- a/solution.py
+++ b/solution.py
@@ -47,13 +47,15 @@
     return lax.optimization_barrier((value, earlier))[0]
 
 
-def scatter_sum(value, axis, flip, start=0):
+def scatter_sum(value, axis, flip, start=0, ties=None):
     rank = lax.axis_index(axis)
     order = bit_order(axis, flip, start)
     bits = len(order)
     value = value.reshape((2,) * bits + (value.shape[0] >> bits, value.shape[1]))
     left = sorted(order, reverse=True)
-    for bit in order:
+    for step, bit in enumerate(order):
+        if ties and step in ties:
+            value = after(value, ties[step])
         at = left.index(bit)
         mine = (rank >> bit) & 1
         send = lax.dynamic_index_in_dim(value, 1 - mine, at, keepdims=False)
@@ -64,26 +66,24 @@
     return value
 
 
-def gather_rows(value, axis, flip, order=None):
-    rank = lax.axis_index(axis)
+def gather_rows(value, axis, flip, ties=None):
     cols = value.shape[1]
-    held = []
-    for bit in reversed(bit_order(axis, flip)) if order is None else order:
-        other = swapped(value, axis, bit)
-        mine = ((rank >> bit) & 1) == 0
-        at = sum(1 for b in held if b > bit)
-        value = jnp.stack([jnp.where(mine, value, other), jnp.where(mine, other, value)], axis=at)
+    ties = ties or {}
+    held, stages = [], []
+    for step, bit in enumerate(reversed(bit_order(axis, flip))):
+        if step in ties:
+            value = after(value, ties[step])
+        value = doubled(value, axis, held, bit)
         held.append(bit)
-    return value.reshape(-1, cols)
-
-
-def gather_pair(value, axis, held, bit):
-    rank = lax.axis_index(axis)
+        stages.append(value)
+    return stages + [value.reshape(-1, cols)]
+
+
+def doubled(value, axis, held, bit):
     other = swapped(value, axis, bit)
-    mine = ((rank >> bit) & 1) == 0
-    at = 1 if held > bit else 0
-    value = jnp.stack([jnp.where(mine, value, other), jnp.where(mine, other, value)], axis=at)
-    return value.reshape(-1, value.shape[-1])
+    mine = ((lax.axis_index(axis) >> bit) & 1) == 0
+    at = sum(1 for b in held if b > bit)
+    return jnp.stack([jnp.where(mine, value, other), jnp.where(mine, other, value)], axis=at)
 
 
 def grouped_columns(value, axis, group):
@@ -229,28 +229,38 @@
     byte_rows = byte_state.shape[0]
     slots = -(-(patch_rows + DRIFT) // 128) * 128
 
-    first = gather_rows(jnp.concatenate([w_key, w_query[:, :half]], axis=1), "seq", False)
-    second = gather_rows(jnp.concatenate([w_value, w_query[:, half:]], axis=1), "seq", True)
+    steps = lax.axis_size("seq").bit_length() - 1
+    group = min(2, steps)
+    rest = steps - group
+    out_half = w_out.shape[1] // 2
+    shared = [out_grad[:, :out_half], out_grad[:, out_half:]]
+    ties = {}
+    held = []
+    for step in range(group):
+        bits = [step, group - 1 - step]
+        shared = [doubled(value, "seq", [h[i] for h in held], bits[i]) for i, value in enumerate(shared)]
+        held.append(bits)
+        ties[rest + step] = list(shared)
+    group_out_grad = jnp.concatenate([value.reshape(-1, out_half) for value in shared], axis=1)
+    first = gather_rows(
+        jnp.concatenate([w_key, w_query[:, :half]], axis=1), "seq", False, ties
+    )
+    second = gather_rows(
+        jnp.concatenate([w_value, w_query[:, half:]], axis=1), "seq", True, ties
+    )
+    ties = {rest: [first[-1], second[-1]]}
+    if rest:
+        ties[0] = [first[rest - 1], second[rest - 1]]
+    first, second = first[-1], second[-1]
+    full_out = jnp.concatenate(
+        [
+            gather_rows(w_out[:, :out_half], "seq", False, ties)[-1],
+            gather_rows(w_out[:, out_half:], "seq", True, ties)[-1],
+        ],
+        axis=1,
+    )
     full_key, full_value = first[:, :width], second[:, :width]
     full_query = jnp.concatenate([first[:, width:], second[:, width:]], axis=1)
-
-    group = min(2, lax.axis_size("seq").bit_length() - 1)
-    out_half = w_out.shape[1] // 2
-    full_out = jnp.concatenate(
-        [
-            gather_rows(after(w_out[:, :out_half], first), "seq", False),
-            gather_rows(after(w_out[:, out_half:], second), "seq", True),
-        ],
-        axis=1,
-    )
-    steps = [list(range(group)), list(range(group))[::-1]]
-    part = [after(out_grad[:, :out_half], full_out), after(out_grad[:, out_half:], full_out)]
-    part = [gather_rows(p, "seq", False, s[:1]) for p, s in zip(part, steps)]
-    shared = [
-        gather_pair(p.reshape(2, patch_rows, out_half), "seq", s[0], s[1]) if group == 2 else p
-        for p, s in zip(part, steps)
-    ]
-    group_out_grad = jnp.concatenate(shared, axis=1)
 
     first_patch = patch_id[0]
     last_patch = patch_id[byte_rows - 1]
@@ -334,7 +344,7 @@
             jax.ShapeDtypeStruct((byte_rows, width), jnp.bfloat16),
             jax.ShapeDtypeStruct((slots, width), jnp.bfloat16),
         ],
-        ids, member_half, query_proj, keys, values, prob, after(slot_grad, part),
+        ids, member_half, query_proj, keys, values, prob, after(slot_grad, grad_out),
     )
     grad_out = jnp.concatenate(
         [
@@ -343,16 +353,21 @@
         ],
         axis=1,
     )
-    grad_key = scatter_sum(contract_rows(byte_state, key_grad), "seq", False)
-    grad_value = scatter_sum(contract_rows(byte_state, value_grad), "seq", True)
-    grad_query = contract_rows(pooled, query_grad)
-    grad_query = jnp.concatenate(
-        [
-            scatter_sum(grad_query[:, :half], "seq", False),
-            scatter_sum(grad_query[:, half:], "seq", True),
-        ],
+    grad_first = jnp.concatenate(
+        [contract_rows(byte_state, key_grad), contract_rows(pooled, query_grad[:, :half])], axis=1
+    )
+    grad_second = jnp.concatenate(
+        [contract_rows(byte_state, value_grad), contract_rows(pooled, query_grad[:, half:])],
         axis=1,
     )
+    key_grad, value_grad, query_grad = lax.optimization_barrier(
+        (key_grad, value_grad, query_grad, grad_first, grad_second)
+    )[:3]
+    ties = {group: grad_out}
+    grad_first = scatter_sum(grad_first, "seq", False, 0, ties)
+    grad_second = scatter_sum(grad_second, "seq", True, 0, ties)
+    grad_key, grad_value = grad_first[:, :width], grad_second[:, :width]
+    grad_query = jnp.concatenate([grad_first[:, width:], grad_second[:, width:]], axis=1)
     pooled_grad = (contract_cols(query_grad, full_query) / length[:, None]).astype(jnp.bfloat16)
     byte_part = (
         contract_cols(key_grad, full_key)

time: 332 us -> 286 us (0.86)
  waiting for transfers between devices: 183 us -> 117 us
  other arithmetic: 23 us -> 39.3 us
    ppermute x45 -> x37, waiting for transfers between devices: 183 us -> 113 us  [swapped(): return lax.ppermute(value, axis, [(i, i ^ 1 << bit) for i in range(count)])]
    another operation x39 -> x37, other arithmetic: 10.7 us -> 19.7 us  [doubled(): jnp.stack([jnp.where(mine, value, other), jnp.where(mine, other, value)],...]
    concatenate x0 -> x2, local copies, waits for them, and re-layouts: none -> 7.17 us  [the longest x1 3.62 us: local(): jnp.concatenate([contract_rows(byte_state, value_grad), contract_rows(poo...]
    dot_general x2 -> x0, local copies, waits for them, and re-layouts: 5.84 us -> none  [contract_rows(): lax.dot_general(left_side, right_side, (((0,), (0,)), ((), ())), preferre...]
    ppermute x2, waiting for transfers between devices: 0.01 us -> 4.24 us  [passed_along(): lax.ppermute(value, axis, [(source, source + steps) for source in range(i...]
    concatenate x1 -> x3, other arithmetic: 0.67 us -> 4.58 us  [the longest x1 2.01 us: local(): jnp.concatenate([contract_rows(byte_state, value_grad), contract_rows(poo...]
    dot_general x7 -> x8, matrix products: 14.2 us -> 12.7 us  [contract_rows(): lax.dot_general(left_side, right_side, (((0,), (0,)), ((), ())), preferre...]
    ppermute x45 -> x37, starting transfers between devices: 59.4 us -> 60.4 us  [swapped(): return lax.ppermute(value, axis, [(i, i ^ 1 << bit) for i in range(count)])]
  transfers between devices with their start and end apart: 47 -> 39, of which waited for: 25 -> 20; matrix products, arithmetic and copies ran while one was open for 18% -> 25% of each run, Pallas kernels for 1% -> 1%
where the time goes in v3:
time: 286 us
  waiting for transfers between devices  117 us (41%)
  starting transfers between devices  64.4 us (23%)
  other arithmetic  39.3 us (14%)
  matrix products  31.2 us (11%)
  local copies, waits for them, and re-layouts  22.7 us (8%)
  Pallas kernels  7.16 us (3%)
  between operations  3.65 us (1%)
    ppermute x37, waiting for transfers between devices, swapped(): return lax.ppermute(value, axis, [(i, i ^ 1 << bit) for i in range(count)])  113 us
    ppermute x37, starting transfers between devices, swapped(): return lax.ppermute(value, axis, [(i, i ^ 1 << bit) for i in range(count)])  60.4 us
    another operation x37, other arithmetic, doubled(): jnp.stack([jnp.where(mine, value, other), jnp.where(mine, other, value)],...  19.7 us
    dot_general x8, matrix products, contract_rows(): lax.dot_general(left_side, right_side, (((0,), (0,)), ((), ())), preferre...  12.7 us
    dot_general x3, matrix products, contract_cols(): lax.dot_general(left_side, right_side, (((1,), (1,)), ((), ())), preferre...  9.98 us
    pallas_call x2, Pallas kernels, run_kernel(): pl.pallas_call(body, out_shape=outs, in_specs=[vmem] * len(operands), out...  7.16 us
    squeeze x12, local copies, waits for them, and re-layouts, scatter_sum(): send = lax.dynamic_index_in_dim(value, 1 - mine, at, keepdims=False)  6.18 us
  transfers between devices with their start and end apart: 39, of which 20 were waited for; matrix products, arithmetic and copies ran while one was open for 25% of the time, Pallas kernels for 1%

profile of v3, /device:TPU:0, one launch (start us, length us, event | category | flops | bytes accessed | tf_op | source)
XLA Modules:
  0.0 285.6 jit_solution(149531884390761886)
XLA Ops:
  2.4 4.0 %collective-permute-start = (bf16[64,768]{1,0:T(8,128)(2,1)S(1)}, bf16[64,768]{1,0:T(8,128)(2,1)}, u32[]{:S(2)}, u32[]{:S(2)}) collective-permute-start(bf16[64,768]{1,0:T(8,128)(2,1)S(1)} %pad_maximum_fusion.40), channel_id=1, source_target_pairs={{0,16},{2,18},{4,20},{6,22},{8,24},{10,26},{12,28},{14,30},{16,0},... | collective-permute-start | bytes 294920 | tf_op jit(solution)/shard_map/ppermute | solution.py:23
  42.2 3.7 %collective-permute-done.10 = bf16[2,2,64,768]{3,2,0,1:T(8,128)(2,1)} collective-permute-done((bf16[2,2,64,768]{3,2,0,1:T(8,128)(2,1)}, bf16[2,2,64,768]{3,2,0,1:T(8,128)(2,1)}, u32[]{:S(2)}, u32[]{:S(2)}) %collective-permute-start.10) | collective-permute-done | bytes 393248 | tf_op jit(solution)/shard_map/ppermute | solution.py:23
  49.6 5.6 %collective-permute-done.5 = bf16[2,224,1024]{2,1,0:T(8,128)(2,1)} collective-permute-done((bf16[2,224,1024]{2,1,0:T(8,128)(2,1)}, bf16[2,224,1024]{2,1,0:T(8,128)(2,1)}, u32[]{:S(2)}, u32[]{:S(2)}) %collective-permute-start.5) | collective-permute-done | bytes 917536 | tf_op jit(solution)/shard_map/ppermute | solution.py:23
  56.5 4.0 %collective-permute-done.6 = bf16[2,224,1024]{2,1,0:T(8,128)(2,1)S(1)} collective-permute-done((bf16[2,224,1024]{2,1,0:T(8,128)(2,1)}, bf16[2,224,1024]{2,1,0:T(8,128)(2,1)S(1)}, u32[]{:S(2)}, u32[]{:S(2)}) %collective-permute-start.6) | collective-permute-done | bytes 917536 | tf_op jit(solution)/shard_map/ppermute | solution.py:23
  68.9 9.0 %collective-permute-done.11 = bf16[2,2,2,64,768]{4,3,0,1,2:T(8,128)(2,1)} collective-permute-done((bf16[2,2,2,64,768]{4,3,0,1,2:T(8,128)(2,1)}, bf16[2,2,2,64,768]{4,3,0,1,2:T(8,128)(2,1)}, u32[]{:S(2)}, u32[]{:S(2)}) %collective-permute-start.11) | collective-permute-done | bytes 786464 | tf_op jit(solution)/shard_map/ppermute | solution.py:23
  84.4 3.3 %shard_map.118 = (f32[8,1024]{1,0:T(8,128)S(1)}, bf16[384,512]{1,0:T(8,128)(2,1)S(1)}) custom-call(s32[1,1024]{1,0:T(1,128)S(1)} %bitcast.191, bf16[384,1024]{1,0:T(8,128)(2,1)S(1)} %fusion.45.member_ref, bf16[384,512]{1,0:T(8,128)(2,1)S(1)} %convolution_convert_fusion.2.query_ref, bf16[1024,512]{1,0:T(8,128)(2,1)S(1)} %fusion.46.key_ref, ...), custom_call_target="tpu_custom_call" | custom-call | flops 8000000000 | bytes 8000000 | tf_op jit(solution)/shard_map/pallas_call | solution.py:209
  99.8 12.8 %collective-permute-done.24 = bf16[1,224,512]{2,1,0:T(8,128)(2,1)S(1)} collective-permute-done((bf16[1,224,512]{2,1,0:T(8,128)(2,1)S(1)}, bf16[1,224,512]{2,1,0:T(8,128)(2,1)S(1)}, u32[]{:S(2)}, u32[]{:S(2)}) %collective-permute-start.24) | collective-permute-done | bytes 229408 | tf_op jit(solution)/shard_map/ppermute | solution.py:23
  116.0 6.1 %collective-permute-done.25 = bf16[2,224,256]{2,1,0:T(8,128)(2,1)S(1)} collective-permute-done((bf16[2,224,256]{2,1,0:T(8,128)(2,1)S(1)}, bf16[2,224,256]{2,1,0:T(8,128)(2,1)S(1)}, u32[]{:S(2)}, u32[]{:S(2)}) %collective-permute-start.25) | collective-permute-done | bytes 229408 | tf_op jit(solution)/shard_map/ppermute | solution.py:23
  123.9 3.5 %collective-permute-start.29 = (f32[2,64,1024]{2,1,0:T(8,128)S(1)}, f32[2,64,1024]{2,1,0:T(8,128)S(1)}, u32[]{:S(2)}, u32[]{:S(2)}) collective-permute-start(f32[2,64,1024]{2,1,0:T(8,128)S(1)} %dynamic-slice_bitcast_fusion.5), channel_id=1, source_target_pairs={{0,8},{2,10},{4,12},{6,14},{8,0},{10,2},{12,4},{14,6},{16,24},{18,... | collective-permute-start | bytes 1572872 | tf_op jit(solution)/shard_map/ppermute | solution.py:23
  130.5 17.6 %collective-permute-done.29 = f32[2,64,1024]{2,1,0:T(8,128)S(1)} collective-permute-done((f32[2,64,1024]{2,1,0:T(8,128)S(1)}, f32[2,64,1024]{2,1,0:T(8,128)S(1)}, u32[]{:S(2)}, u32[]{:S(2)}) %collective-permute-start.29) | collective-permute-done | bytes 524320 | tf_op jit(solution)/shard_map/ppermute | solution.py:23
  148.6 9.6 %collective-permute-start.32 = (f32[64,1024]{1,0:T(8,128)S(1)}, f32[64,1024]{1,0:T(8,128)S(1)}, u32[]{:S(2)}, u32[]{:S(2)}) collective-permute-start(f32[64,1024]{1,0:T(8,128)S(1)} %dynamic-slice_bitcast_fusion.8), channel_id=1, source_target_pairs={{0,8},{2,10},{4,12},{6,14},{8,0},{10,2},{12,4},{14,6},{16,24},{18,... | collective-permute-start | bytes 786440 | tf_op jit(solution)/shard_map/ppermute | solution.py:23
  165.9 4.0 %collective-permute-done.23 = bf16[56,512]{1,0:T(8,128)(2,1)S(1)} collective-permute-done((bf16[56,512]{1,0:T(8,128)(2,1)S(1)}, bf16[56,512]{1,0:T(8,128)(2,1)S(1)}, u32[]{:S(2)}, u32[]{:S(2)}) %collective-permute-start.23) | collective-permute-done | bytes 57376 | tf_op jit(solution)/shard_map/ppermute | solution.py:18
  170.6 3.8 %shard_map.119 = (bf16[1024,512]{1,0:T(8,128)(2,1)S(1)}, bf16[1024,512]{1,0:T(8,128)(2,1)S(1)}, bf16[384,512]{1,0:T(8,128)(2,1)S(1)}) custom-call(s32[1,1024]{1,0:T(1,128)S(1)} %bitcast.192, bf16[384,1024]{1,0:T(8,128)(2,1)S(1)} %copy-done.4, bf16[384,512]{1,0:T(8,128)(2,1)S(1)} %convolution_convert_fusion.2.query_ref, ...), custom_call_target="tpu_custom_call" | custom-call | flops 8000000000 | bytes 8000000 | tf_op jit(solution)/shard_map/pallas_call | solution.py:209
  182.3 3.6 %copy.40 = f32[1024,768]{1,0:T(8,128)} copy(f32[1024,768]{0,1:T(8,128)} %pad_maximum_fusion.2) | data formatting | bytes 6291456 | tf_op jit(solution)/shard_map/concatenate | solution.py:359
  191.3 3.5 %copy.39 = f32[1024,768]{1,0:T(8,128)} copy(f32[1024,768]{0,1:T(8,128)} %pad_maximum_fusion.1) | data formatting | bytes 6291456 | tf_op jit(solution)/shard_map/concatenate | solution.py:356
  200.8 3.3 %fusion.58 = f32[1024,1024]{1,0:T(8,128)} fusion(bf16[1024,512]{1,0:T(8,128)(2,1)S(1)} %copy-done.2, bf16[1024,768]{1,0:T(8,128)(2,1)S(1)} %bitcast.206), kind=kOutput, calls=%fused_computation.103 | convolution fusion | flops 1073741824 | bytes 6291456 | tf_op jit(solution)/shard_map/dot_general | solution.py:27
  204.1 4.9 %fusion.43 = f32[1024,1024]{1,0:T(8,128)} fusion(bf16[384,512]{1,0:T(8,128)(2,1)S(1)} %get-tuple-element.41, f32[384]{0:T(512)S(1)} %copy-done.49, s32[1024]{0:T(1024)S(1)} %broadcast_subtract_fusion, bf16[1024,256]{1,0:T(8,128)(2,1)} %copy-done.29, bf16[1024,256]{1,0:T(8,128)(2,1)} %copy-done.30), kind=kOutput, calls=%fused_computation.80 | convolution fusion | flops 1211236352 | bytes 5641728 | tf_op jit(solution)/shard_map/dot_general | solution.py:33
  209.1 5.3 %add_convert_fusion.1 = bf16[1024,1024]{1,0:T(8,128)(2,1)S(1)} fusion(f32[1024,1024]{1,0:T(8,128)} %fusion.43, f32[1024,1024]{1,0:T(8,128)} %fusion.58, bf16[1024,512]{1,0:T(8,128)(2,1)S(1)} %get-tuple-element.40, bf16[1024,768]{1,0:T(8,128)(2,1)} %bitcast.199), kind=kOutput, calls=%fused_computation.33 | convolution fusion | flops 1076887552 | bytes 12582912 | tf_op jit(solution)/shard_map/dot_general | solution.py:27
  214.4 10.0 %collective-permute-done.35 = f32[2,2,2,64,768]{4,3,2,1,0:T(8,128)} collective-permute-done((f32[2,2,2,64,768]{4,3,2,1,0:T(8,128)}, f32[2,2,2,64,768]{4,3,2,1,0:T(8,128)}, u32[]{:S(2)}, u32[]{:S(2)}) %collective-permute-start.35) | collective-permute-done | bytes 1572896 | tf_op jit(solution)/shard_map/ppermute | solution.py:23
  228.0 8.4 %collective-permute-done.27 = f32[2,2,2,64,768]{4,3,2,1,0:T(8,128)} collective-permute-done((f32[2,2,2,64,768]{4,3,2,1,0:T(8,128)}, f32[2,2,2,64,768]{4,3,2,1,0:T(8,128)}, u32[]{:S(2)}, u32[]{:S(2)}) %collective-permute-start.27) | collective-permute-done | bytes 1572896 | tf_op jit(solution)/shard_map/ppermute | solution.py:23
  242.1 9.0 %collective-permute-done.36 = f32[2,2,64,768]{3,2,1,0:T(8,128)S(1)} collective-permute-done((f32[2,2,64,768]{3,2,1,0:T(8,128)S(1)}, f32[2,2,64,768]{3,2,1,0:T(8,128)S(1)}, u32[]{:S(2)}, u32[]{:S(2)}) %collective-permute-start.36) | collective-permute-done | bytes 786464 | tf_op jit(solution)/shard_map/ppermute | solution.py:23
  258.9 6.6 %collective-permute-done.37 = f32[2,64,768]{2,1,0:T(8,128)S(1)} collective-permute-done((f32[2,64,768]{2,1,0:T(8,128)S(1)}, f32[2,64,768]{2,1,0:T(8,128)S(1)}, u32[]{:S(2)}, u32[]{:S(2)}) %collective-permute-start.37) | collective-permute-done | bytes 393248 | tf_op jit(solution)/shard_map/ppermute | solution.py:23
  267.0 6.6 %collective-permute-done.33 = f32[2,64,768]{2,1,0:T(8,128)S(1)} collective-permute-done((f32[2,64,768]{2,1,0:T(8,128)S(1)}, f32[2,64,768]{2,1,0:T(8,128)S(1)}, u32[]{:S(2)}, u32[]{:S(2)}) %collective-permute-start.33) | collective-permute-done | bytes 393248 | tf_op jit(solution)/shard_map/ppermute | solution.py:23
  275.4 5.0 %collective-permute-done.38 = f32[64,768]{1,0:T(8,128)S(1)} collective-permute-done((f32[64,768]{1,0:T(8,128)S(1)}, f32[64,768]{1,0:T(8,128)S(1)}, u32[]{:S(2)}, u32[]{:S(2)}) %collective-permute-start.38) | collective-permute-done | bytes 196640 | tf_op jit(solution)/shard_map/ppermute | solution.py:23
  (288 shorter events, 128.5 us)
Async XLA Ops:
  2.4 21.0 %collective-permute-start = (bf16[64,768]{1,0:T(8,128)(2,1)S(1)}, bf16[64,768]{1,0:T(8,128)(2,1)}, u32[]{:S(2)}, u32[]{:S(2)}) collective-permute-start(bf16[64,768]{1,0:T(8,128)(2,1)S(1)} %pad_maximum_fusion.40), channel_id=1, source_target_pairs={{0,16},{2,18},{4,20},{6,22},{8,24},{10,26},{12,28},{14,30},{16,0},... | collective-permute-start | bytes 294920 | tf_op jit(solution)/shard_map/ppermute | solution.py:23
  9.5 20.1 %collective-permute-start.3 = (bf16[224,1024]{1,0:T(8,128)(2,1)}, bf16[224,1024]{1,0:T(8,128)(2,1)}, u32[]{:S(2)}, u32[]{:S(2)}) collective-permute-start(bf16[224,1024]{1,0:T(8,128)(2,1)} %get-tuple-element.68), channel_id=1, source_target_pairs={{0,4},{2,6},{4,0},{6,2},{8,12},{10,14},{12,8},{14,10},{16,20},{18,... | collective-permute-start | bytes 1376264 | tf_op jit(solution)/shard_map/ppermute | solution.py:23
  11.3 18.2 %collective-permute-start.2 = (bf16[224,1024]{1,0:T(8,128)(2,1)}, bf16[224,1024]{1,0:T(8,128)(2,1)}, u32[]{:S(2)}, u32[]{:S(2)}) collective-permute-start(bf16[224,1024]{1,0:T(8,128)(2,1)} %get-tuple-element.69), channel_id=1, source_target_pairs={{0,2},{2,0},{4,6},{6,4},{8,10},{10,8},{12,14},{14,12},{16,18},{18,... | collective-permute-start | bytes 1376264 | tf_op jit(solution)/shard_map/ppermute | solution.py:23
  32.0 23.1 %collective-permute-start.5 = (bf16[2,224,1024]{2,1,0:T(8,128)(2,1)}, bf16[2,224,1024]{2,1,0:T(8,128)(2,1)}, u32[]{:S(2)}, u32[]{:S(2)}) collective-permute-start(bf16[2,224,1024]{2,1,0:T(8,128)(2,1)} %pad_maximum_fusion.18), channel_id=1, source_target_pairs={{0,4},{2,6},{4,0},{6,2},{8,12},{10,14},{12,8},{14,10},{16,20},{18,... | collective-permute-start | bytes 2752520 | tf_op jit(solution)/shard_map/ppermute | solution.py:23
  35.7 24.8 %collective-permute-start.6 = (bf16[2,224,1024]{2,1,0:T(8,128)(2,1)}, bf16[2,224,1024]{2,1,0:T(8,128)(2,1)S(1)}, u32[]{:S(2)}, u32[]{:S(2)}) collective-permute-start(bf16[2,224,1024]{2,1,0:T(8,128)(2,1)} %pad_maximum_fusion.19), channel_id=1, source_target_pairs={{0,2},{2,0},{4,6},{6,4},{8,10},{10,8},{12,14},{14,12},{16,18},{18,... | collective-permute-start | bytes 2752520 | tf_op jit(solution)/shard_map/ppermute | solution.py:23
  39.2 25.1 %collective-permute-start.18 = (bf16[64,1024]{1,0:T(8,128)(2,1)}, bf16[64,1024]{1,0:T(8,128)(2,1)S(1)}, u32[]{:S(2)}, u32[]{:S(2)}) collective-permute-start(bf16[64,1024]{1,0:T(8,128)(2,1)} %get-tuple-element.32), channel_id=1, source_target_pairs={{0,16},{2,18},{4,20},{6,22},{8,24},{10,26},{12,28},{14,30},{16,0},... | collective-permute-start | bytes 393224 | tf_op jit(solution)/shard_map/ppermute | solution.py:23
  41.8 22.6 %collective-permute-start.14 = (bf16[64,1024]{1,0:T(8,128)(2,1)}, bf16[64,1024]{1,0:T(8,128)(2,1)}, u32[]{:S(2)}, u32[]{:S(2)}) collective-permute-start(bf16[64,1024]{1,0:T(8,128)(2,1)} %get-tuple-element.30), channel_id=1, source_target_pairs={{0,16},{2,18},{4,20},{6,22},{8,24},{10,26},{12,28},{14,30},{16,0},... | collective-permute-start | bytes 393224 | tf_op jit(solution)/shard_map/ppermute | solution.py:23
  45.9 21.1 %collective-permute-start.4 = (bf16[2,2,64,768]{3,2,1,0:T(8,128)(2,1)}, bf16[2,2,64,768]{3,2,1,0:T(8,128)(2,1)}, u32[]{:S(2)}, u32[]{:S(2)}) collective-permute-start(bf16[2,2,64,768]{3,2,1,0:T(8,128)(2,1)} %pad_maximum_fusion.30), channel_id=1, source_target_pairs={{0,4},{2,6},{4,0},{6,2},{8,12},{10,14},{12,8},{14,10},{16,20},{18,... | collective-permute-start | bytes 1179656 | tf_op jit(solution)/shard_map/ppermute | solution.py:23
  62.8 15.0 %collective-permute-start.11 = (bf16[2,2,2,64,768]{4,3,0,1,2:T(8,128)(2,1)}, bf16[2,2,2,64,768]{4,3,0,1,2:T(8,128)(2,1)}, u32[]{:S(2)}, u32[]{:S(2)}) collective-permute-start(bf16[2,2,2,64,768]{4,3,0,1,2:T(8,128)(2,1)} %pad_maximum_fusion.21), channel_id=1, source_target_pairs={{0,4},{2,6},{4,0},{6,2},{8,12},{10,14},{12,8},{14,10},{16,20},{18,... | collective-permute-start | bytes 2359304 | tf_op jit(solution)/shard_map/ppermute | solution.py:23
  65.4 27.2 %collective-permute-start.19 = (bf16[2,64,1024]{2,1,0:T(8,128)(2,1)S(1)}, bf16[2,64,1024]{2,1,0:T(8,128)(2,1)S(1)}, u32[]{:S(2)}, u32[]{:S(2)}) collective-permute-start(bf16[2,64,1024]{2,1,0:T(8,128)(2,1)S(1)} %pad_maximum_fusion.35), channel_id=1, source_target_pairs={{0,8},{2,10},{4,12},{6,14},{8,0},{10,2},{12,4},{14,6},{16,24},{18,... | collective-permute-start | bytes 786440 | tf_op jit(solution)/shard_map/ppermute | solution.py:23
  92.7 22.9 %collective-permute-start.20 = (bf16[2,2,64,1024]{3,2,0,1:T(8,128)(2,1)S(1)}, bf16[2,2,64,1024]{3,2,0,1:T(8,128)(2,1)S(1)}, u32[]{:S(2)}, u32[]{:S(2)}) collective-permute-start(bf16[2,2,64,1024]{3,2,0,1:T(8,128)(2,1)S(1)} %pad_maximum_fusion.26), channel_id=1, source_target_pairs={{0,2},{2,0},{4,6},{6,4},{8,10},{10,8},{12,14},{14,12},{16,18},{18,... | collective-permute-start | bytes 1572872 | tf_op jit(solution)/shard_map/ppermute | solution.py:23
  96.5 16.2 %collective-permute-start.24 = (bf16[1,224,512]{2,1,0:T(8,128)(2,1)S(1)}, bf16[1,224,512]{2,1,0:T(8,128)(2,1)S(1)}, u32[]{:S(2)}, u32[]{:S(2)}) collective-permute-start(bf16[1,224,512]{2,1,0:T(8,128)(2,1)S(1)} %broadcast_select_fusion.3), channel_id=1, source_target_pairs={{0,2},{2,0},{4,6},{6,4},{8,10},{10,8},{12,14},{14,12},{16,18},{18,... | collective-permute-start | bytes 688136 | tf_op jit(solution)/shard_map/ppermute | solution.py:23
  97.9 32.1 %collective-permute-start.16 = (bf16[2,2,64,1024]{3,2,1,0:T(8,128)(2,1)S(1)}, bf16[2,2,64,1024]{3,2,1,0:T(8,128)(2,1)S(1)}, u32[]{:S(2)}, u32[]{:S(2)}) collective-permute-start(bf16[2,2,64,1024]{3,2,1,0:T(8,128)(2,1)S(1)} %pad_maximum_fusion.25), channel_id=1, source_target_pairs={{0,4},{2,6},{4,0},{6,2},{8,12},{10,14},{12,8},{14,10},{16,20},{18,... | collective-permute-start | bytes 1572872 | tf_op jit(solution)/shard_map/ppermute | solution.py:23
  115.9 42.3 %collective-permute-start.21 = (bf16[2,2,2,64,1024]{4,3,0,1,2:T(8,128)(2,1)S(1)}, bf16[2,2,2,64,1024]{4,3,0,1,2:T(8,128)(2,1)S(1)}, u32[]{:S(2)}, u32[]{:S(2)}) collective-permute-start(bf16[2,2,2,64,1024]{4,3,0,1,2:T(8,128)(2,1)S(1)} %pad_maximum_fusion.17), channel_id=1, source_target_pairs={{0,4},{2,6},{4,0},{6,2},{8,12},{10,14},{12,8},{14,10},{16,20},{18,... | collective-permute-start | bytes 3145736 | tf_op jit(solution)/shard_map/ppermute | solution.py:23
  123.9 24.3 %collective-permute-start.29 = (f32[2,64,1024]{2,1,0:T(8,128)S(1)}, f32[2,64,1024]{2,1,0:T(8,128)S(1)}, u32[]{:S(2)}, u32[]{:S(2)}) collective-permute-start(f32[2,64,1024]{2,1,0:T(8,128)S(1)} %dynamic-slice_bitcast_fusion.5), channel_id=1, source_target_pairs={{0,8},{2,10},{4,12},{6,14},{8,0},{10,2},{12,4},{14,6},{16,24},{18,... | collective-permute-start | bytes 1572872 | tf_op jit(solution)/shard_map/ppermute | solution.py:23
  127.4 21.1 %collective-permute-start.31 = (f32[2,64,1024]{2,1,0:T(8,128)S(1)}, f32[2,64,1024]{2,1,0:T(8,128)S(1)}, u32[]{:S(2)}, u32[]{:S(2)}) collective-permute-start(f32[2,64,1024]{2,1,0:T(8,128)S(1)} %dynamic-slice_bitcast_fusion.4), channel_id=1, source_target_pairs={{0,16},{2,18},{4,20},{6,22},{8,24},{10,26},{12,28},{14,30},{16,0},... | collective-permute-start | bytes 1572872 | tf_op jit(solution)/shard_map/ppermute | solution.py:23
  130.2 28.5 %collective-permute-start.17 = (bf16[2,2,2,64,1024]{4,3,2,1,0:T(8,128)(2,1)S(1)}, bf16[2,2,2,64,1024]{4,3,2,1,0:T(8,128)(2,1)S(1)}, u32[]{:S(2)}, u32[]{:S(2)}) collective-permute-start(bf16[2,2,2,64,1024]{4,3,2,1,0:T(8,128)(2,1)S(1)} %pad_maximum_fusion.16), channel_id=1, source_target_pairs={{0,2},{2,0},{4,6},{6,4},{8,10},{10,8},{12,14},{14,12},{16,18},{18,... | collective-permute-start | bytes 3145736 | tf_op jit(solution)/shard_map/ppermute | solution.py:23
  148.6 16.6 %collective-permute-start.32 = (f32[64,1024]{1,0:T(8,128)S(1)}, f32[64,1024]{1,0:T(8,128)S(1)}, u32[]{:S(2)}, u32[]{:S(2)}) collective-permute-start(f32[64,1024]{1,0:T(8,128)S(1)} %dynamic-slice_bitcast_fusion.8), channel_id=1, source_target_pairs={{0,8},{2,10},{4,12},{6,14},{8,0},{10,2},{12,4},{14,6},{16,24},{18,... | collective-permute-start | bytes 786440 | tf_op jit(solution)/shard_map/ppermute | solution.py:23
  188.8 35.6 %collective-permute-start.35 = (f32[2,2,2,64,768]{4,3,2,1,0:T(8,128)}, f32[2,2,2,64,768]{4,3,2,1,0:T(8,128)}, u32[]{:S(2)}, u32[]{:S(2)}) collective-permute-start(f32[2,2,2,64,768]{4,3,2,1,0:T(8,128)} %dynamic-slice_bitcast_fusion), channel_id=1, source_target_pairs={{0,4},{2,6},{4,0},{6,2},{8,12},{10,14},{12,8},{14,10},{16,20},{18,... | collective-permute-start | bytes 4718600 | tf_op jit(solution)/shard_map/ppermute | solution.py:23
  197.8 38.7 %collective-permute-start.27 = (f32[2,2,2,64,768]{4,3,2,1,0:T(8,128)}, f32[2,2,2,64,768]{4,3,2,1,0:T(8,128)}, u32[]{:S(2)}, u32[]{:S(2)}) collective-permute-start(f32[2,2,2,64,768]{4,3,2,1,0:T(8,128)} %dynamic-slice_bitcast_fusion.1), channel_id=1, source_target_pairs={{0,2},{2,0},{4,6},{6,4},{8,10},{10,8},{12,14},{14,12},{16,18},{18,... | collective-permute-start | bytes 4718600 | tf_op jit(solution)/shard_map/ppermute | solution.py:23
  214.4 42.3 %collective-permute-start.26 = (bf16[1024,1024]{1,0:T(8,128)(2,1)S(1)}, bf16[1024,1024]{1,0:T(8,128)(2,1)S(1)}, u32[]{:S(2)}, u32[]{:S(2)}) collective-permute-start(bf16[1024,1024]{1,0:T(8,128)(2,1)S(1)} %add_convert_fusion.1), channel_id=1, source_target_pairs={{0,1},{1,0},{2,3},{3,2},{4,5},{5,4},{6,7},{7,6},{8,9},{9,8},{10,11... | collective-permute-start | bytes 6291464 | tf_op jit(solution)/shard_map/ppermute | solution.py:23
  226.1 25.1 %collective-permute-start.36 = (f32[2,2,64,768]{3,2,1,0:T(8,128)S(1)}, f32[2,2,64,768]{3,2,1,0:T(8,128)S(1)}, u32[]{:S(2)}, u32[]{:S(2)}) collective-permute-start(f32[2,2,64,768]{3,2,1,0:T(8,128)S(1)} %dynamic-slice_bitcast_fusion.2), channel_id=1, source_target_pairs={{0,2},{2,0},{4,6},{6,4},{8,10},{10,8},{12,14},{14,12},{16,18},{18,... | collective-permute-start | bytes 2359304 | tf_op jit(solution)/shard_map/ppermute | solution.py:23
  238.3 15.5 %collective-permute-start.28 = (f32[2,2,64,768]{3,2,1,0:T(8,128)S(1)}, f32[2,2,64,768]{3,2,1,0:T(8,128)S(1)}, u32[]{:S(2)}, u32[]{:S(2)}) collective-permute-start(f32[2,2,64,768]{3,2,1,0:T(8,128)S(1)} %dynamic-slice_bitcast_fusion.3), channel_id=1, source_target_pairs={{0,4},{2,6},{4,0},{6,2},{8,12},{10,14},{12,8},{14,10},{16,20},{18,... | collective-permute-start | bytes 2359304 | tf_op jit(solution)/shard_map/ppermute | solution.py:23
  254.0 19.5 %collective-permute-start.33 = (f32[2,64,768]{2,1,0:T(8,128)S(1)}, f32[2,64,768]{2,1,0:T(8,128)S(1)}, u32[]{:S(2)}, u32[]{:S(2)}) collective-permute-start(f32[2,64,768]{2,1,0:T(8,128)S(1)} %dynamic-slice_bitcast_fusion.7), channel_id=1, source_target_pairs={{0,8},{2,10},{4,12},{6,14},{8,0},{10,2},{12,4},{14,6},{16,24},{18,... | collective-permute-start | bytes 1179656 | tf_op jit(solution)/shard_map/ppermute | solution.py:23
  (69 other events, 526.2 us)
